TPU v7x, 512 devices: a whole 4x8x8 slice. The times are simulated.
512 devices in a mesh: user: 32 (over x, z), seq: 16 (over y, core).
Axes of the slice: x: 4, y: 8, z: 8, core: 2. Of those that a mesh axis runs over, the one named last changes fastest.
Arguments:
- hist_feat: bfloat16 [32, 2048, 1024], P('user', 'seq'), may hold values from -6 to 6
- hist_length: int32 [32], P('user'), may hold values from 512 to 2048, as said below
- time_bucket: int32 [32, 2048], P('user', 'seq'), may hold values from 0 to 31
- cand_feat: bfloat16 [16384, 1024], P(('user', 'seq')), may hold values from -6 to 6
- cand_owner: int32 [16384, 1], P(('user', 'seq')), may hold values from 0 to 31; in each aligned block of 32 rows (0 to 31, 32 to 63, ...) at most 2 rows name the same one
- proj_weight: bfloat16 [1024, 16, 256], P(None, 'seq'), may hold values from -0.1875 to 0.1875
- time_bias: float32 [16, 32], replicated, may hold values from -4 to 4
- norm_gain: float32 [1024], replicated, may hold values from 0.1 to 1.9
- out_weight: bfloat16 [1024, 1024], replicated, may hold values from -0.1875 to 0.1875
Outputs:
- hist_out: bfloat16 [32, 2048, 1024], P('user', 'seq')
- cand_out: bfloat16 [16384, 1024], P(('user', 'seq'))
Inputs may be any that keep to these rules, and one draw needn't show every extreme that they name: `hist_length`: some user's history has exactly 2048 valid events; events at or beyond a user's length are padding. `cand_owner`: the 32 candidate rows of one device name one user at most 2 times, and some device names some user exactly 2 times.
All inputs are finite; a program needn't handle non-finite values.
Results may differ from a plain program's by a relative error of at most 0.0058.
Values may be sent and summed in bfloat16 or wider, within the bound.
A program may use at most 64 MiB of HBM per device.

v0:
```python
import math

import jax
import jax.numpy as jnp
from jax import lax
from jax.sharding import PartitionSpec as P

norm_eps = 1e-05


def project_rows(row_block, weight):
    projected = jnp.einsum("rd,dhe->rhe", row_block, weight, preferred_element_type=jnp.float32)
    return jax.nn.silu(projected).astype(jnp.bfloat16)


def finish_rows(attention, gate_vals, inputs, norm_gain, out_weight):
    row_total = inputs.shape[0]
    attn_flat = attention.reshape(row_total, -1).astype(jnp.float32)
    row_mean = jnp.mean(attn_flat, axis=1, keepdims=True)
    centred = attn_flat - row_mean
    row_var = jnp.mean(centred * centred, axis=1, keepdims=True)
    gated_rows = (
        centred
        * lax.rsqrt(row_var + norm_eps)
        * norm_gain
        * gate_vals.reshape(row_total, -1).astype(jnp.float32)
    ).astype(jnp.bfloat16)
    result = jnp.dot(gated_rows, out_weight, preferred_element_type=jnp.float32) + inputs.astype(
        jnp.float32
    )
    return result.astype(jnp.bfloat16)


def body(
    hist_feat,
    hist_length,
    time_bucket,
    cand_feat,
    cand_owner,
    proj_weight,
    time_bias,
    norm_gain,
    out_weight,
):
    user_count = lax.axis_size("user")
    seq_count = lax.axis_size("seq")
    hist_rows = hist_feat[0]
    hist_dev = hist_rows.shape[0]
    model_width = hist_rows.shape[1]
    cand_dev = cand_feat.shape[0]
    capacity = 2 * cand_dev // user_count
    owner_ids = cand_owner[:, 0]
    same_owner = owner_ids[:, None] == owner_ids[None, :]
    earlier = lax.broadcasted_iota(jnp.int32, (cand_dev, cand_dev), 1) < lax.broadcasted_iota(
        jnp.int32, (cand_dev, cand_dev), 0
    )
    slot_rank = jnp.sum(jnp.where(same_owner & earlier, 1, 0), axis=1).astype(jnp.int32)
    slot_index = owner_ids * capacity + slot_rank
    send_buffer = (
        jnp.zeros((user_count * capacity, model_width), cand_feat.dtype)
        .at[slot_index]
        .set(cand_feat)
    )
    arrived = lax.all_to_all(
        send_buffer.reshape(user_count, capacity, model_width),
        "user",
        split_axis=0,
        concat_axis=0,
        tiled=True,
    )
    local_rows = jnp.concatenate(
        [hist_rows, arrived.reshape(user_count * capacity, model_width)], axis=0
    )
    row_count = local_rows.shape[0]
    local_heads = proj_weight.shape[1]
    head_size = proj_weight.shape[2] // 4
    projected = project_rows(local_rows, lax.all_gather(proj_weight, "seq", axis=1, tiled=True))
    gate_local = projected[:, :, :head_size]
    head_major = lax.all_to_all(
        projected[:, :, head_size:], "seq", split_axis=1, concat_axis=0, tiled=True
    )
    value_all = head_major[:, :, :head_size]
    query_all = head_major[:, :, head_size : 2 * head_size]
    key_all = head_major[:, :, 2 * head_size :]
    total_rows = seq_count * row_count
    hist_total = seq_count * hist_dev

    def history_part(source):
        shaped = source.reshape(seq_count, row_count, local_heads, head_size)
        return shaped[:, :hist_dev].reshape(hist_total, local_heads, head_size)

    key_hist = history_part(key_all)
    value_hist = history_part(value_all)
    buckets = lax.all_gather(time_bucket[0], "seq", axis=0, tiled=True)
    bucket_count = time_bias.shape[1]
    bias_mine = lax.dynamic_slice_in_dim(
        time_bias, lax.axis_index("seq") * local_heads, local_heads, 0
    )
    bucket_hit = buckets[:, None] == lax.broadcasted_iota(jnp.int32, (hist_total, bucket_count), 1)
    key_bias = jnp.sum(jnp.where(bucket_hit[None], bias_mine[:, None, :], 0.0), axis=2)
    row_ids = jnp.arange(total_rows, dtype=jnp.int32)
    source_dev = row_ids // row_count
    within = row_ids % row_count
    limits = jnp.where(within < hist_dev, source_dev * hist_dev + within, hist_total - 1)
    key_pos = jnp.arange(hist_total, dtype=jnp.int32)
    length = hist_length[0]
    score_scale = head_size ** (-0.5)
    block_rows = math.gcd(total_rows, 512)

    def one_block(block_index):
        first_row = block_index * block_rows
        queries = lax.dynamic_slice_in_dim(query_all, first_row, block_rows, 0)
        block_limit = lax.dynamic_slice_in_dim(limits, first_row, block_rows, 0)
        scores = (
            jnp.einsum("qhd,khd->hqk", queries, key_hist, preferred_element_type=jnp.float32)
            * score_scale
            + key_bias[:, None, :]
        )
        keep_mask = (key_pos[None, :] <= block_limit[:, None]) & (key_pos[None, :] < length)
        weights = jnp.where(keep_mask[None], jax.nn.silu(scores), 0.0).astype(jnp.bfloat16)
        return jnp.einsum(
            "hqk,khd->qhd", weights, value_hist, preferred_element_type=jnp.float32
        ).astype(jnp.bfloat16)

    attention = lax.map(one_block, jnp.arange(total_rows // block_rows, dtype=jnp.int32))
    attention = attention.reshape(total_rows, local_heads, head_size)
    attn_rows = lax.all_to_all(attention, "seq", split_axis=0, concat_axis=1, tiled=True)
    mixed_rows = finish_rows(attn_rows, gate_local, local_rows, norm_gain, out_weight)
    hist_out = mixed_rows[:hist_dev][None]
    returned = lax.all_to_all(
        mixed_rows[hist_dev:].reshape(user_count, capacity, model_width),
        "user",
        split_axis=0,
        concat_axis=0,
        tiled=True,
    )
    cand_out = returned.reshape(user_count * capacity, model_width)[slot_index]
    return (hist_out, cand_out)


def solution(mesh):
    in_specs = (
        P("user", "seq", None),
        P("user"),
        P("user", "seq"),
        P(("user", "seq"), None),
        P(("user", "seq"), None),
        P(None, "seq", None),
        P(),
        P(),
        P(),
    )
    out_specs = (P("user", "seq", None), P(("user", "seq"), None))
    return jax.shard_map(body, mesh=mesh, in_specs=in_specs, out_specs=out_specs, check_vma=False)
```

profile of v0, /device:TPU:1, one launch (start us, length us, event | category | flops | bytes accessed | tf_op | source)
XLA Modules:
  0.0 291.8 jit_solution(10756014224967074177)
XLA Ops:
  10.6 22.7 %all_to_all.37 = bf16[32,2,1024]{2,1,0:T(2,128)(2,1)S(1)} all-to-all(bf16[32,2,1024]{2,1,0:T(2,128)(2,1)S(1)} %reshape.153), channel_id=1, replica_groups=mesh['user'=32,'seq'=16] {'user'}, dimensions={0} | all-to-all | bytes 262144 | tf_op jit(solution)/shard_map/all_to_all | solution.py:64
  33.4 40.9 %all-gather.3.cloned.1.call-done = bf16[1024,16,256]{2,0,1:T(8,128)(2,1)} async-done(((bf16[1024,1,256]{2,0,1:T(8,128)(2,1)}), bf16[1024,16,256]{2,0,1:T(8,128)(2,1)}) %all-gather.3.cloned.1.call-update) | async-done | bytes 8388624 | tf_op jit(solution)/shard_map/all_gather | solution.py:77
  74.3 7.0 %multiply_convert_fusion = bf16[192,16,256]{0,2,1:T(8,128)(2,1)S(1)} fusion(bf16[1024,16,256]{2,0,1:T(8,128)(2,1)} %all-gather.3.cloned.1.call-done, bf16[64,1024]{1,0:T(8,128)(2,1)S(1)} %reshape.154, bf16[128,1024]{1,0:T(8,128)(2,1)} %bitcast.95), kind=kOutput, calls=%fused_computation.19 | convolution fusion | flops 1615331328 | bytes 10354688 | tf_op jit(solution)/shard_map/rd,dhe->rhe/dot_general | solution.py:12
  84.0 4.7 %all-to-all-start.1 = ((bf16[192,16,192]{0,2,1:T(8,128)(2,1)}), bf16[192,16,192]{0,2,1:T(8,128)(2,1)}, u32[]{:S(2)}, u32[]{:S(2)}) async-start(bf16[192,16,192]{0,2,1:T(8,128)(2,1)} %slice.38), calls=%async_computation.1 | async-start | bytes 3145728 | tf_op jit(solution)/shard_map/all_to_all | solution.py:79
  88.8 48.1 %all-gather = s32[1,2048]{1,0:T(1,128)S(1)} all-gather(s32[1,128]{1,0:T(1,128)S(1)} %copy-done.4), channel_id=2, replica_groups=mesh['user'=32,'seq'=16] {'seq'}, dimensions={1}, use_global_device_ids=true | all-gather | bytes 8704 | tf_op jit(solution)/shard_map/all_gather | solution.py:94
  137.7 3.5 %copy.39 = bf16[16,192,1,192]{1,0,3,2:T(8,128)(2,1)} copy(bf16[16,192,1,192]{1,3,0,2:T(8,128)(2,1)} %bitcast.7) | data formatting | bytes 2359296 | tf_op jit(solution)/shard_map/all_to_all | solution.py:79
  141.2 3.0 %all_to_all.30 = bf16[3072,1,192]{0,2,1:T(8,128)(2,1)S(1)} reshape(bf16[16,192,1,192]{1,0,3,2:T(8,128)(2,1)} %copy.39) | data formatting | bytes 2359296 | tf_op jit(solution)/shard_map/all_to_all | solution.py:79
  148.8 34.0 %while.12 = (s32[]{:T(128)}, bf16[6,512,1,64]{1,3,2,0:T(8,128)(2,1)}, s32[6]{0:T(128)S(1)}, s32[3072]{0:T(1024)S(1)}, s32[]{:T(128)}, /*index=5*/bf16[3072,1,64]...) while((s32[]{:T(128)}, ...), condition=%wide.region_4.5_spmd.clone.clone, body=%wide.region_3.4_spmd.clone.clone.sunk | while | flops 278956032 | bytes 674499 | solution.py:125
  150.8 3.7 %fusion.51 = bf16[6,512,1,64]{1,3,2,0:T(8,128)(2,1)} fusion(bf16[6,512,1,64]{1,3,2,0:T(8,128)(2,1)} %get-tuple-element.192, s32[]{:T(128)} %get-tuple-element.191, f32[2048]{0:T(1024)S(1)} %bitcast.99, s32[512]{0:T(512)S(1)} %dynamic_slice.31, pred[2048]{0:T(1024)(128)(4,1)S(1)} %iota_compare_fusion.5, ...), kind=kOutput, calls=%fused_computation.9.clone.1 | convolution fusion | flops 278953984 | bytes 668164 | tf_op jit(solution)/shard_map/while/body/eval_jaxpr/hqk,khd->qhd/dot_general | solution.py:121
  156.5 3.7 %fusion.51 = bf16[6,512,1,64]{1,3,2,0:T(8,128)(2,1)} fusion(bf16[6,512,1,64]{1,3,2,0:T(8,128)(2,1)} %get-tuple-element.192, s32[]{:T(128)} %get-tuple-element.191, f32[2048]{0:T(1024)S(1)} %bitcast.99, s32[512]{0:T(512)S(1)} %dynamic_slice.31, pred[2048]{0:T(1024)(128)(4,1)S(1)} %iota_compare_fusion.5, ...), kind=kOutput, calls=%fused_computation.9.clone.1 | convolution fusion | flops 278953984 | bytes 668164 | tf_op jit(solution)/shard_map/while/body/eval_jaxpr/hqk,khd->qhd/dot_general | solution.py:121
  162.1 3.7 %fusion.51 = bf16[6,512,1,64]{1,3,2,0:T(8,128)(2,1)} fusion(bf16[6,512,1,64]{1,3,2,0:T(8,128)(2,1)} %get-tuple-element.192, s32[]{:T(128)} %get-tuple-element.191, f32[2048]{0:T(1024)S(1)} %bitcast.99, s32[512]{0:T(512)S(1)} %dynamic_slice.31, pred[2048]{0:T(1024)(128)(4,1)S(1)} %iota_compare_fusion.5, ...), kind=kOutput, calls=%fused_computation.9.clone.1 | convolution fusion | flops 278953984 | bytes 668164 | tf_op jit(solution)/shard_map/while/body/eval_jaxpr/hqk,khd->qhd/dot_general | solution.py:121
  167.8 3.7 %fusion.51 = bf16[6,512,1,64]{1,3,2,0:T(8,128)(2,1)} fusion(bf16[6,512,1,64]{1,3,2,0:T(8,128)(2,1)} %get-tuple-element.192, s32[]{:T(128)} %get-tuple-element.191, f32[2048]{0:T(1024)S(1)} %bitcast.99, s32[512]{0:T(512)S(1)} %dynamic_slice.31, pred[2048]{0:T(1024)(128)(4,1)S(1)} %iota_compare_fusion.5, ...), kind=kOutput, calls=%fused_computation.9.clone.1 | convolution fusion | flops 278953984 | bytes 668164 | tf_op jit(solution)/shard_map/while/body/eval_jaxpr/hqk,khd->qhd/dot_general | solution.py:121
  173.4 3.7 %fusion.51 = bf16[6,512,1,64]{1,3,2,0:T(8,128)(2,1)} fusion(bf16[6,512,1,64]{1,3,2,0:T(8,128)(2,1)} %get-tuple-element.192, s32[]{:T(128)} %get-tuple-element.191, f32[2048]{0:T(1024)S(1)} %bitcast.99, s32[512]{0:T(512)S(1)} %dynamic_slice.31, pred[2048]{0:T(1024)(128)(4,1)S(1)} %iota_compare_fusion.5, ...), kind=kOutput, calls=%fused_computation.9.clone.1 | convolution fusion | flops 278953984 | bytes 668164 | tf_op jit(solution)/shard_map/while/body/eval_jaxpr/hqk,khd->qhd/dot_general | solution.py:121
  179.1 3.7 %fusion.51 = bf16[6,512,1,64]{1,3,2,0:T(8,128)(2,1)} fusion(bf16[6,512,1,64]{1,3,2,0:T(8,128)(2,1)} %get-tuple-element.192, s32[]{:T(128)} %get-tuple-element.191, f32[2048]{0:T(1024)S(1)} %bitcast.99, s32[512]{0:T(512)S(1)} %dynamic_slice.31, pred[2048]{0:T(1024)(128)(4,1)S(1)} %iota_compare_fusion.5, ...), kind=kOutput, calls=%fused_computation.9.clone.1 | convolution fusion | flops 278953984 | bytes 668164 | tf_op jit(solution)/shard_map/while/body/eval_jaxpr/hqk,khd->qhd/dot_general | solution.py:121
  184.2 2.4 reshape.189
  187.1 18.0 %reduce.7 = bf16[3072,64]{1,0:T(8,128)(2,1)S(1)} reduce(bf16[3072,1,64]{2,1,0:T(2,128)(2,1)} %reshape.189, bf16[]{:T(256)} %broadcast.133), dimensions={1}, to_apply=%reshape.189.reduce_sub_computation | reduce | bytes 786434 | tf_op jit(solution)/shard_map/reshape | solution.py:126
  206.4 6.0 %all-to-all-start.2 = ((bf16[16,2,6144]{2,1,0:T(2,128)(2,1)}), bf16[16,2,6144]{2,1,0:T(2,128)(2,1)S(1)}, u32[]{:S(2)}, u32[]{:S(2)}) async-start(bf16[16,2,6144]{2,1,0:T(2,128)(2,1)} %reshape.192), calls=%async_computation.2 | async-start | bytes 786432 | tf_op jit(solution)/shard_map/all_to_all | solution.py:127
  214.3 12.7 %all-to-all-done.2 = bf16[16,2,6144]{2,1,0:T(2,128)(2,1)S(1)} async-done(((bf16[16,2,6144]{2,1,0:T(2,128)(2,1)}), bf16[16,2,6144]{2,1,0:T(2,128)(2,1)S(1)}, u32[]{:S(2)}, u32[]{:S(2)}) %all-to-all-start.2) | async-done | bytes 393248 | tf_op jit(solution)/shard_map/all_to_all | solution.py:127
  226.9 2.1 reshape.193
  229.0 4.3 %convert_element_type.74 = f32[3072,1,64]{2,1,0:T(1,128)} convert(bf16[3072,1,64]{2,1,0:T(2,128)(2,1)} %reshape.193) | non-fusion elementwise | flops 196608 | bytes 1179648 | tf_op jit(solution)/shard_map/convert_element_type | solution.py:18
  233.3 22.8 %convert_reduce_fusion = f32[3072]{0:T(1024)S(1)} fusion(bf16[3072,1,64]{2,1,0:T(2,128)(2,1)S(1)} %copy-done.1), kind=kLoop, calls=%fused_computation.61 | loop fusion | flops 390144 | bytes 405504 | tf_op jit(solution)/shard_map/reduce_sum | solution.py:19
  256.3 2.0 copy.42
  263.8 9.9 %all-to-all-start.3 = ((bf16[32,2,1024]{2,1,0:T(2,128)(2,1)}), bf16[32,2,1024]{2,1,0:T(2,128)(2,1)S(1)}, u32[]{:S(2)}, u32[]{:S(2)}) async-start(bf16[32,2,1024]{2,1,0:T(2,128)(2,1)} %reshape.160), calls=%async_computation.3 | async-start | bytes 262144 | tf_op jit(solution)/shard_map/all_to_all | solution.py:130
  274.5 9.2 %all-to-all-done.3 = bf16[32,2,1024]{2,1,0:T(2,128)(2,1)S(1)} async-done(((bf16[32,2,1024]{2,1,0:T(2,128)(2,1)}), bf16[32,2,1024]{2,1,0:T(2,128)(2,1)S(1)}, u32[]{:S(2)}, u32[]{:S(2)}) %all-to-all-start.3) | async-done | bytes 131104 | tf_op jit(solution)/shard_map/all_to_all | solution.py:130
  (66 shorter events, 32.2 us)
Async XLA Ops:
  7.2 254.4 %copy-start = (bf16[1024,1024]{1,0:T(8,128)(2,1)S(1)}, bf16[1024,1024]{1,0:T(8,128)(2,1)}, u32[]{:S(2)}) copy-start(bf16[1024,1024]{1,0:T(8,128)(2,1)} %param.19) | copy-start | bytes 6291460
  7.2 67.1 %all-gather.3.cloned.1.call-start = ((), (), s32[]{:S(2)}) async-start(), calls=%async_computation.4 | async-start | bytes 8912896 | tf_op jit(solution)/shard_map/all_gather | solution.py:77
  81.3 1.4 copy-start.2
  82.7 6.1 %copy-start.4 = (s32[1,128]{1,0:T(1,128)S(1)}, s32[1,128]{1,0:T(1,128)}, u32[]{:S(2)}) copy-start(s32[1,128]{1,0:T(1,128)} %param.13) | copy-start | bytes 1540
  84.0 53.7 %all-to-all-start.1 = ((bf16[192,16,192]{0,2,1:T(8,128)(2,1)}), bf16[192,16,192]{0,2,1:T(8,128)(2,1)}, u32[]{:S(2)}, u32[]{:S(2)}) async-start(bf16[192,16,192]{0,2,1:T(8,128)(2,1)} %slice.38), calls=%async_computation.1 | async-start | bytes 3145728 | tf_op jit(solution)/shard_map/all_to_all | solution.py:79
  206.4 20.5 %all-to-all-start.2 = ((bf16[16,2,6144]{2,1,0:T(2,128)(2,1)}), bf16[16,2,6144]{2,1,0:T(2,128)(2,1)S(1)}, u32[]{:S(2)}, u32[]{:S(2)}) async-start(bf16[16,2,6144]{2,1,0:T(2,128)(2,1)} %reshape.192), calls=%async_computation.2 | async-start | bytes 786432 | tf_op jit(solution)/shard_map/all_to_all | solution.py:127
  229.0 4.3 %copy-start.1 = (bf16[3072,1,64]{2,1,0:T(2,128)(2,1)S(1)}, bf16[3072,1,64]{2,1,0:T(2,128)(2,1)}, u32[]{:S(2)}) copy-start(bf16[3072,1,64]{2,1,0:T(2,128)(2,1)} %reshape.193) | copy-start | bytes 1179652
  229.0 31.0 %copy-start.3 = (f32[1024]{0:T(1024)S(1)}, f32[1024]{0:T(1024)}, u32[]{:S(2)}) copy-start(f32[1024]{0:T(1024)} %param.18) | copy-start | bytes 12292
  263.8 19.8 %all-to-all-start.3 = ((bf16[32,2,1024]{2,1,0:T(2,128)(2,1)}), bf16[32,2,1024]{2,1,0:T(2,128)(2,1)S(1)}, u32[]{:S(2)}, u32[]{:S(2)}) async-start(bf16[32,2,1024]{2,1,0:T(2,128)(2,1)} %reshape.160), calls=%async_computation.3 | async-start | bytes 262144 | tf_op jit(solution)/shard_map/all_to_all | solution.py:130
Sparse Core Ops, SparseCore 0:
  10.1 64.1 all-gather.2
where the time goes:
time: 293 us; the launch traced here: 292 us
  blocking collectives  70.8 us (24%)
  waiting for transfers between devices  63.5 us (22%)
  other arithmetic  54 us (18%)
  local copies, waits for them, and re-layouts  34 us (12%)
  matrix products  30.7 us (10%)
  starting transfers between devices  20.6 us (7%)
  between operations  14.2 us (5%)
  loops' own time  4 us (1%)
    all_gather x1, blocking collectives, body(): buckets = lax.all_gather(time_bucket[0], 'seq', axis=0, tiled=True)  48.1 us
    all_gather x1, waiting for transfers between devices, body(): lax.all_gather(proj_weight, 'seq', axis=1, tiled=True)  40.9 us
    reduce_sum x2, other arithmetic, finish_rows(): row_mean = jnp.mean(attn_flat, axis=1, keepdims=True)  22.9 us
    all_to_all x1, blocking collectives, body(): lax.all_to_all(send_buffer.reshape(user_count, capacity, model_width), 'u...  22.7 us
    dot_general x6, matrix products, one_block(): jnp.einsum('hqk,khd->qhd', weights, value_hist, preferred_element_type=jn...  22.1 us
    reshape x1, other arithmetic, body(): attention = attention.reshape(total_rows, local_heads, head_size)  18 us
    all_to_all x1, waiting for transfers between devices, body(): lax.all_to_all(attention, 'seq', split_axis=0, concat_axis=1, tiled=True)  12.7 us
    all_to_all x1, starting transfers between devices, body(): lax.all_to_all(mixed_rows[hist_dev:].reshape(user_count, capacity, model_...  9.89 us
  transfers between devices with their start and end apart: 4, of which 3 were waited for; matrix products, arithmetic and copies ran while one was open for 2% of the time, Pallas kernels for 0%

commit v1 on v0

v1 whole, which is shorter than its diff:
```python
import functools

import jax
import jax.numpy as jnp
from jax import lax
from jax.experimental import pallas as pl
from jax.experimental.pallas import tpu as pltpu
from jax.sharding import PartitionSpec as P

MESH = pl.DeviceIdType.MESH
NORM_EPS = 1e-05
NX, NZ, NY = 4, 8, 8
NU, NS = NX * NZ, NY * 2
D = 1024
DH = 64
NB = 32
HR = 128
CR = 64
HIST = HR * NS
PAY_V = 2 * HR
PAY_Q = 3 * HR
PAY_B = 3 * HR + CR
PAY = PAY_B + 16
F32 = jnp.float32
BF16 = jnp.bfloat16


def dot(a, b):
    return jnp.dot(a, b, preferred_element_type=F32)


def dot_nt(a, b):
    return lax.dot_general(a, b, (((1,), (1,)), ((), ())), preferred_element_type=F32)


def iota(shape, axis):
    return lax.broadcasted_iota(jnp.int32, shape, axis)


def half_silu(h):
    return h * jnp.tanh(h) + h


def swap(a):
    return pltpu.roll(a, DH, axis=1)


def low_lanes(rows):
    return iota((rows, 128), 1) < DH


def join(lo, hi):
    return jnp.where(low_lanes(lo.shape[0]), lo, swap(hi))


def kernel(
    hist_in,
    length_in,
    bucket_in,
    cand_in,
    owner_in,
    weight_in,
    bias_in,
    gain_in,
    out_w_in,
    hist_out,
    cand_out,
    feats,
    weights,
    out_w,
    bucket_own,
    bucket_sib,
    cand_stack,
    cand_send,
    cand_arr,
    pay,
    got,
    gate_own,
    gate_send,
    gate_sib,
    queries,
    keys,
    values,
    back_c,
    back_h,
    arr_c,
    arr_h,
    done_stack,
    done_send,
    done_arr,
    local_sem,
    ring_s,
    ring_r,
    side_s,
    side_r,
    diag_s,
    diag_r,
    cand_s,
    cand_r,
    pay_s,
    pay_r,
    sib_s,
    sib_r,
    back_cs,
    back_cr,
    back_hs,
    back_hr,
    done_s,
    done_r,
):
    user = lax.axis_index("user")
    seq = lax.axis_index("seq")
    x, z = user // NZ, user % NZ
    y, core = seq // 2, seq % 2
    part = (x + z) % 4
    sibling = (user, y * 2 + (1 - core))

    def along_y(step):
        return (user, ((y + NY + step) % NY) * 2 + core)

    def along_x(step):
        return (((x + NX + step) % NX) * NZ + z, seq)

    def along_z(step):
        return (x * NZ + (z + NZ + step) % NZ, seq)

    def remote(src, dst, send, recv, to):
        return pltpu.make_async_remote_copy(
            src_ref=src, dst_ref=dst, send_sem=send, recv_sem=recv, device_id=to, device_id_type=MESH
        )

    own_weight = pltpu.make_async_copy(weight_in, weights.at[y], local_sem.at[0])
    own_feats = pltpu.make_async_copy(hist_in, feats.at[pl.ds(0, HR)], local_sem.at[1])
    own_out_w = pltpu.make_async_copy(out_w_in, out_w, local_sem.at[2])
    own_weight.start()
    own_feats.start()
    own_out_w.start()

    barrier = pltpu.get_barrier_semaphore()

    def greet_user(t, carry):
        pl.semaphore_signal(barrier, inc=1, device_id=((user + t) % NU, seq), device_id_type=MESH)
        return carry

    def greet_seq(t, carry):
        pl.semaphore_signal(barrier, inc=1, device_id=(user, (seq + t) % NS), device_id_type=MESH)
        return carry

    lax.fori_loop(1, NU, greet_user, 0)
    lax.fori_loop(1, NS, greet_seq, 0)

    lane = iota((32, 128), 1)
    row = iota((32, 128), 0)
    owner_row = jnp.concatenate([owner_in[...].astype(F32), jnp.zeros((1, 96), F32)], axis=1)
    owner_wide = jnp.broadcast_to(owner_row, (32, 128))
    owner_col = jnp.sum(jnp.where(lane == row, owner_wide, 0.0), axis=1, keepdims=True)
    same = (owner_wide == owner_col) & (lane < 32)
    rank_row = jnp.sum(jnp.where(same & (row < lane), 1.0, 0.0), axis=0, keepdims=True)
    rank_col = jnp.sum(jnp.where(same & (lane < row), 1.0, 0.0), axis=1, keepdims=True)
    slot_row = owner_row * 2.0 + rank_row
    slot_col = owner_col * 2.0 + rank_col
    spread = jnp.where(iota((128, 256), 0) == iota((128, 256), 1) % 32, 1.0, 0.0).astype(BF16)
    slot_wide = dot(jnp.broadcast_to(slot_row, (16, 128)).astype(BF16), spread)[0:1]
    for k in range(8):
        cand_stack[32 * k : 32 * k + 32, :] = cand_in[:, 128 * k : 128 * k + 128]
    m_row = iota((512, 256), 0)
    place = jnp.where(
        (m_row % 8 == iota((512, 256), 1) // 32) & ((m_row // 8).astype(F32) == slot_wide), 1.0, 0.0
    )
    cand_send[...] = dot(place.astype(BF16), cand_stack[...]).astype(BF16)
    bucket_own[...] = jnp.broadcast_to(bucket_in[...].astype(F32), (16, 128)).astype(BF16)

    pl.semaphore_wait(barrier, NU - 1 + NS - 1)

    sent = []

    def go(copy):
        copy.start()
        sent.append(copy)

    def quarter(origin, cls, half, at=0, rows=128):
        start = pl.multiple_of(cls * 256 + half * 128 + at, 64)
        return weights.at[origin, pl.ds(start, rows)]

    def ring_copy(dirn, step, half, src):
        sign = 1 if dirn == 0 else -1
        origin = (y + NY - sign * (step - 1)) % NY
        dst = quarter(origin, part, half)
        return remote(
            dst if src is None else src,
            dst,
            ring_s.at[dirn, step - 1, half],
            ring_r.at[dirn, step - 1, half],
            along_y(sign),
        )

    for half in range(2):
        start = pl.multiple_of(part * 256 + half * 128, 128)
        for dirn in range(2):
            go(ring_copy(dirn, 1, half, weight_in.at[pl.ds(start, 128)]))
    go(remote(hist_in, feats.at[pl.ds(HR, HR)], sib_s.at[0], sib_r.at[0], sibling))
    go(remote(bucket_own, bucket_sib, sib_s.at[1], sib_r.at[1], sibling))

    def cand_copy(t):
        to = (user + t) % NU
        return remote(
            cand_send.at[pl.ds(pl.multiple_of(to * 16, 16), 16)],
            cand_arr.at[pl.ds(pl.multiple_of(user * 16, 16), 16)],
            cand_s.at[t],
            cand_r.at[t],
            (to, seq),
        )

    def cand_start(t, carry):
        cand_copy(t).start()
        return carry

    lax.fori_loop(1, NU, cand_start, 0)
    mine = pl.ds(pl.multiple_of(user * 16, 16), 16)
    own_cand = pltpu.make_async_copy(cand_send.at[mine], cand_arr.at[mine], local_sem.at[3])
    own_cand.start()

    def origin_of(dirn, step):
        sign = 1 if dirn == 0 else -1
        return (y + NY - sign * step) % NY

    def index_of(dirn, step):
        return 2 * (step - 1) + (dirn if step < 4 else 0)

    def side_copy(dirn, step, axis, way):
        origin = origin_of(dirn, step)
        sign = 1 if way == 0 else -1
        ref = quarter(origin, part, axis)
        to = along_x(sign) if axis == 0 else along_z(sign)
        o = index_of(dirn, step)
        return remote(ref, ref, side_s.at[o, axis, way], side_r.at[o, axis, way], to)

    def diag_copy(dirn, step, axis, way):
        origin = origin_of(dirn, step)
        sign = 1 if way == 0 else -1
        ref = quarter(origin, (part + 4 - sign) % 4, axis, 64 * way, 64)
        to = along_x(sign) if axis == 0 else along_z(sign)
        o = index_of(dirn, step)
        return remote(ref, ref, diag_s.at[o, axis, way], diag_r.at[o, axis, way], to)

    def ring_step(step):
        for half in range(2):
            for dirn in range(2):
                if step == 4 and dirn != half:
                    continue
                ring_copy(dirn, step, half, None).wait_recv()
                if step < 3 or (step == 3 and dirn == half):
                    go(ring_copy(dirn, step + 1, half, None))
                for way in range(2):
                    go(side_copy(dirn, step, half, way))

    def side_step(step):
        for axis in range(2):
            for dirn in range(2 if step < 4 else 1):
                for way in range(2):
                    side_copy(dirn, step, axis, way).wait_recv()
                    go(diag_copy(dirn, step, axis, way))

    def diag_step(step):
        for axis in range(2):
            for dirn in range(2 if step < 4 else 1):
                for way in range(2):
                    diag_copy(dirn, step, axis, way).wait_recv()

    is_first = core == 0

    def project(origin, slot):
        acc = dot(feats[...], weights[origin])
        full = half_silu(acc * 0.5)
        gv, qk = full[:, 0:128], full[:, 128:256]
        gvb = gv.astype(BF16)
        gate_own[origin, 0:HR] = gvb[0:HR]
        gate_own[origin, HR : HR + CR] = gvb[2 * HR : 2 * HR + CR]
        gate_send[origin, 0:HR] = gvb[HR : 2 * HR]
        gate_send[origin, HR : HR + CR] = gvb[2 * HR + CR : 2 * HR + 2 * CR]
        at_own = pl.multiple_of(core * HR, HR)
        at_sib = pl.multiple_of((1 - core) * HR, HR)
        pay[slot, pl.ds(at_own, HR)] = qk[0:HR].astype(BF16)
        pay[slot, pl.ds(at_sib, HR)] = qk[HR : 2 * HR].astype(BF16)
        low = low_lanes(HR)
        own_v, sib_v = gv[0:HR], gv[HR : 2 * HR]
        v_pair = jnp.where(
            is_first, jnp.where(low, swap(own_v), sib_v), jnp.where(low, swap(sib_v), own_v)
        )
        pay[slot, PAY_V : PAY_V + HR] = v_pair.astype(BF16)
        own_q, sib_q = qk[2 * HR : 2 * HR + CR], qk[2 * HR + CR : 2 * HR + 2 * CR]
        q_pair = jnp.where(is_first, join(own_q, sib_q), join(sib_q, own_q))
        pay[slot, PAY_Q : PAY_Q + CR] = q_pair.astype(BF16)
        first = iota((16, 128), 0) == core
        pay[slot, PAY_B : PAY_B + 16] = jnp.where(
            first, bucket_own[...].astype(F32), bucket_sib[...].astype(F32)
        ).astype(BF16)

    def pay_copy(rel):
        to = (y + rel) % NY
        return remote(pay.at[rel], got.at[y], pay_s.at[rel], pay_r.at[rel], (user, to * 2 + core))

    def project_step(step):
        def one(k, carry):
            rel = jnp.where(k == 0, step, NY - step)
            project((y + rel) % NY, rel)
            pay_copy(rel).start()
            return carry

        lax.fori_loop(0, 2 if step < 4 else 1, one, 0)

    ring_step(1)

    def cand_wait(t, carry):
        cand_copy(t).wait_recv()
        return carry

    lax.fori_loop(1, NU, cand_wait, 0)
    own_cand.wait()
    col = iota((512, 512), 1)
    to_slots = jnp.where(col == 8 * (iota((512, 512), 0) % 64) + iota((512, 512), 0) // 64, 1.0, 0.0)
    slots = dot(to_slots.astype(BF16), cand_arr[...]).astype(BF16)
    for k in range(8):
        feats[2 * HR : 2 * HR + CR, 128 * k : 128 * k + 128] = slots[64 * k : 64 * k + 64]
    go(
        remote(
            feats.at[pl.ds(2 * HR, CR)],
            feats.at[pl.ds(2 * HR + CR, CR)],
            sib_s.at[2],
            sib_r.at[2],
            sibling,
        )
    )
    side_step(1)
    ring_step(2)

    own_feats.wait()
    own_weight.wait()
    remote(hist_in, feats.at[pl.ds(HR, HR)], sib_s.at[0], sib_r.at[0], sibling).wait_recv()
    remote(bucket_own, bucket_sib, sib_s.at[1], sib_r.at[1], sibling).wait_recv()
    remote(
        feats.at[pl.ds(2 * HR, CR)],
        feats.at[pl.ds(2 * HR + CR, CR)],
        sib_s.at[2],
        sib_r.at[2],
        sibling,
    ).wait_recv()
    project(y, 0)
    own_pay = pltpu.make_async_copy(pay.at[0], got.at[y], local_sem.at[4])
    own_pay.start()
    side_step(2)
    ring_step(3)
    diag_step(1)
    project_step(1)
    side_step(3)
    ring_step(4)
    diag_step(2)
    project_step(2)
    side_step(4)
    diag_step(3)
    project_step(3)
    diag_step(4)
    project_step(4)
    gate_copy = remote(gate_send, gate_sib, sib_s.at[3], sib_r.at[3], sibling)
    go(gate_copy)

    head_sel = iota((16, 128), 0) == seq
    table = jnp.concatenate([bias_in[...], jnp.zeros((16, 96), F32)], axis=1) * 0.5
    bias_row = jnp.sum(jnp.where(head_sel, table, 0.0), axis=0, keepdims=True)
    bias_hi = bias_row.astype(BF16).astype(F32)
    bias_lo = bias_row - bias_hi
    bias_lanes = pltpu.roll(jnp.broadcast_to(bias_hi, (8, 128)), DH, axis=1) + pltpu.roll(
        jnp.broadcast_to(bias_lo, (8, 128)), DH + NB, axis=1
    )
    bias_lanes = bias_lanes[0:1]
    length = length_in[0]

    own_pay.wait()

    def pay_wait(t, carry):
        pay_copy(t).wait_recv()
        return carry

    lax.fori_loop(1, NY, pay_wait, 0)

    low = low_lanes(HR)
    lane_h = iota((HR, 128), 1)
    row_h = iota((HR, 128), 0)

    def prepare(src, carry):
        v_pair = got[src, PAY_V : PAY_V + HR].astype(F32)
        v_swap = swap(v_pair)
        buckets = got[src, PAY_B : PAY_B + 16].astype(F32)
        base = src * (2 * HR)
        for c in range(2):
            qk = got[src, c * HR : c * HR + HR].astype(F32)
            at = pl.multiple_of(base + c * HR, HR)
            queries[pl.ds(at, HR)] = jnp.where(low, qk * 0.0625, bias_lanes).astype(BF16)
            mine_b = jnp.sum(jnp.where(lane_h == row_h, buckets[c : c + 1], 0.0), axis=1, keepdims=True)
            hit = jnp.where((lane_h % NB).astype(F32) == mine_b, 1.0, 0.0)
            keys[pl.ds(at, HR)] = jnp.where(low, swap(qk), hit).astype(BF16)
            v = jnp.where(low, v_pair, v_swap) if c == 0 else jnp.where(low, v_swap, v_pair)
            values[pl.ds(at, HR)] = jnp.where(row_h + at < length, v, 0.0).astype(BF16)
        q_pair = got[src, PAY_Q : PAY_Q + CR].astype(F32)
        low_c = low_lanes(CR)
        at = pl.multiple_of(HIST + src * HR, HR)
        queries[pl.ds(at, CR)] = jnp.where(low_c, q_pair * 0.0625, bias_lanes).astype(BF16)
        queries[pl.ds(at + CR, CR)] = jnp.where(low_c, swap(q_pair) * 0.0625, bias_lanes).astype(BF16)
        return carry

    lax.fori_loop(0, NY, prepare, 0)

    def attend(q, acc, at, width, mask=None):
        h = dot_nt(q, keys[pl.ds(at, width)])
        w = half_silu(h)
        if mask is not None:
            w = jnp.where(mask, w, 0.0)
        return acc + dot(w.astype(BF16), values[pl.ds(at, width)])

    def back_c_copy(to):
        return remote(
            back_c.at[to], arr_c.at[seq], back_cs.at[to], back_cr.at[seq], (user, to)
        )

    def back_h_copy(to):
        return remote(
            back_h.at[to], arr_h.at[seq], back_hs.at[to], back_hr.at[seq], (user, to)
        )

    def send_back(to, copy, out, arr):
        @pl.when(to != seq)
        def _():
            copy(to).start()

        @pl.when(to == seq)
        def _():
            arr[seq] = out

    def cand_block(i, carry):
        q = queries[pl.ds(pl.multiple_of(HIST + i * 256, 256), 256)]
        acc = jnp.zeros((256, 128), F32)
        for j in range(4):
            acc = attend(q, acc, 512 * j, 512)
        for c in range(4):
            o = acc[c * CR : c * CR + CR]
            packed = jnp.where(low_lanes(CR // 2), o[0 : CR // 2], o[CR // 2 : CR]).astype(BF16)
            to = i * 4 + c
            back_c[to] = packed
            send_back(to, back_c_copy, packed, arr_c)
        return carry

    lax.fori_loop(0, 4, cand_block, 0)

    tri = iota((256, 256), 1) <= iota((256, 256), 0)
    for i in range(8):
        q = queries[i * 256 : i * 256 + 256]
        acc = jnp.zeros((256, 128), F32)
        for j in range(i // 2):
            acc = attend(q, acc, 512 * j, 512)
        if i % 2:
            acc = attend(q, acc, (i - 1) * 256, 256)
        acc = attend(q, acc, i * 256, 256, tri)
        for c in range(2):
            o = acc[c * HR : c * HR + HR]
            packed = jnp.where(low_lanes(HR // 2), o[0 : HR // 2], o[HR // 2 : HR]).astype(BF16)
            to = i * 2 + c
            back_h[to] = packed
            send_back(to, back_h_copy, packed, arr_h)

    def wait_back(copy_sem, arr, back):
        def one(t, carry):
            src = (seq + t) % NS
            remote(back.at[src], arr.at[src], copy_sem[0].at[src], copy_sem[1].at[src], (user, src)).wait_recv()
            return carry

        lax.fori_loop(1, NS, one, 0)

    def finish(arr, rows, at, inputs):
        half = rows // 2
        low_half, low_rows = low_lanes(half), low_lanes(rows)
        tiles, total = [], jnp.zeros((rows, 128), F32)
        for p in range(NY):
            even, odd = arr[2 * p].astype(F32), arr[2 * p + 1].astype(F32)
            tile = jnp.concatenate(
                [jnp.where(low_half, even, swap(odd)), jnp.where(low_half, swap(even), odd)], axis=0
            )
            tiles.append(tile)
            total = total + tile
        mean = jnp.sum(total, axis=1, keepdims=True) * (1.0 / D)
        tiles = [t - mean for t in tiles]
        squares = jnp.zeros((rows, 128), F32)
        for t in tiles:
            squares = squares + t * t
        var = jnp.sum(squares, axis=1, keepdims=True) * (1.0 / D)
        scale = lax.rsqrt(var + NORM_EPS)
        gated = []
        for p in range(NY):
            own = gate_own[p, at : at + rows].astype(F32)
            sib = gate_sib[p, at : at + rows].astype(F32)
            even, odd = jnp.where(is_first, own, sib), jnp.where(is_first, sib, own)
            gate = jnp.where(low_rows, even, swap(odd))
            g = tiles[p] * scale * gain_in[:, 128 * p : 128 * p + 128] * gate
            gated.append(g.astype(BF16))
        result = dot(jnp.concatenate(gated, axis=1), out_w[...])
        return (result + inputs.astype(F32)).astype(BF16)

    gate_copy.wait_recv()
    own_out_w.wait()
    wait_back((back_cs, back_cr), arr_c, back_c)
    cand_done = finish(arr_c, CR, HR, feats[2 * HR : 2 * HR + CR])
    for k in range(8):
        done_stack[64 * k : 64 * k + 64] = cand_done[:, 128 * k : 128 * k + 128]
    r512 = iota((512, 512), 0)
    from_slots = jnp.where(r512 == 8 * (col % 64) + col // 64, 1.0, 0.0)
    done_send[...] = dot(from_slots.astype(BF16), done_stack[...]).astype(BF16)

    def done_copy(t):
        to = (user + t) % NU
        return remote(
            done_send.at[pl.ds(pl.multiple_of(to * 16, 16), 16)],
            done_arr.at[pl.ds(pl.multiple_of(user * 16, 16), 16)],
            done_s.at[t],
            done_r.at[t],
            (to, seq),
        )

    def done_start(t, carry):
        done_copy(t).start()
        return carry

    lax.fori_loop(1, NU, done_start, 0)
    own_done = pltpu.make_async_copy(done_send.at[mine], done_arr.at[mine], local_sem.at[5])
    own_done.start()

    wait_back((back_hs, back_hr), arr_h, back_h)
    hist_out[...] = finish(arr_h, HR, 0, feats[0:HR])

    def done_wait(t, carry):
        done_copy(t).wait_recv()
        return carry

    lax.fori_loop(1, NU, done_wait, 0)
    own_done.wait()
    slot_tall = jnp.concatenate([slot_col] * 8, axis=0)
    pick = jnp.where(
        iota((256, 512), 1).astype(F32) == slot_tall * 8.0 + (iota((256, 512), 0) // 32).astype(F32), 1.0, 0.0
    )
    picked = dot(pick.astype(BF16), done_arr[...]).astype(BF16)
    for k in range(8):
        cand_out[:, 128 * k : 128 * k + 128] = picked[32 * k : 32 * k + 32]

    for copy in sent:
        copy.wait_send()

    def user_sends(t, carry):
        cand_copy(t).wait_send()
        done_copy(t).wait_send()
        return carry

    def pay_sends(t, carry):
        pay_copy(t).wait_send()
        return carry

    def back_sends(t, carry):
        to = (seq + t) % NS
        back_c_copy(to).wait_send()
        back_h_copy(to).wait_send()
        return carry

    lax.fori_loop(1, NU, user_sends, 0)
    lax.fori_loop(1, NY, pay_sends, 0)
    lax.fori_loop(1, NS, back_sends, 0)


def body(hist, length, bucket, cand, owner, weight, bias, gain, out_weight):
    vmem = pl.BlockSpec(memory_space=pltpu.VMEM)
    hbm = pl.BlockSpec(memory_space=pl.ANY)
    smem = pl.BlockSpec(memory_space=pltpu.SMEM)
    dma = pltpu.SemaphoreType.DMA
    hist_out, cand_out = pl.pallas_call(
        kernel,
        out_shape=(
            jax.ShapeDtypeStruct((HR, D), BF16),
            jax.ShapeDtypeStruct((32, D), BF16),
        ),
        in_specs=[hbm, smem, vmem, vmem, vmem, hbm, vmem, vmem, hbm],
        out_specs=(vmem, vmem),
        scratch_shapes=[
            pltpu.VMEM((2 * HR + 2 * CR, D), BF16),
            pltpu.VMEM((NY, D, 4 * DH), BF16),
            pltpu.VMEM((D, D), BF16),
            pltpu.VMEM((16, 128), BF16),
            pltpu.VMEM((16, 128), BF16),
            pltpu.VMEM((256, 128), BF16),
            pltpu.VMEM((512, 128), BF16),
            pltpu.VMEM((512, 128), BF16),
            pltpu.VMEM((NY, PAY, 128), BF16),
            pltpu.VMEM((NY, PAY, 128), BF16),
            pltpu.VMEM((NY, HR + CR, 128), BF16),
            pltpu.VMEM((NY, HR + CR, 128), BF16),
            pltpu.VMEM((NY, HR + CR, 128), BF16),
            pltpu.VMEM((HIST + NS * CR, 128), BF16),
            pltpu.VMEM((HIST, 128), BF16),
            pltpu.VMEM((HIST, 128), BF16),
            pltpu.VMEM((NS, CR // 2, 128), BF16),
            pltpu.VMEM((NS, HR // 2, 128), BF16),
            pltpu.VMEM((NS, CR // 2, 128), BF16),
            pltpu.VMEM((NS, HR // 2, 128), BF16),
            pltpu.VMEM((512, 128), BF16),
            pltpu.VMEM((512, 128), BF16),
            pltpu.VMEM((512, 128), BF16),
            dma((6,)),
            dma((2, 4, 2)),
            dma((2, 4, 2)),
            dma((7, 2, 2)),
            dma((7, 2, 2)),
            dma((7, 2, 2)),
            dma((7, 2, 2)),
            dma((NU,)),
            dma((NU,)),
            dma((NY,)),
            dma((NY,)),
            dma((4,)),
            dma((4,)),
            dma((NS,)),
            dma((NS,)),
            dma((NS,)),
            dma((NS,)),
            dma((NU,)),
            dma((NU,)),
        ],
        compiler_params=pltpu.CompilerParams(
            collective_id=0, has_side_effects=True, vmem_limit_bytes=48 * 1024 * 1024
        ),
        cost_estimate=pl.CostEstimate(
            flops=4 * 10**9, bytes_accessed=8 * 10**6, transcendentals=5 * 10**6
        ),
    )(
        hist.reshape(HR, D),
        length,
        bucket,
        cand,
        owner.reshape(1, 32),
        weight.reshape(D, 4 * DH),
        bias,
        gain.reshape(1, D),
        out_weight,
    )
    return hist_out.reshape(1, HR, D), cand_out


def solution(mesh):
    in_specs = (
        P("user", "seq", None),
        P("user"),
        P("user", "seq"),
        P(("user", "seq"), None),
        P(("user", "seq"), None),
        P(None, "seq", None),
        P(),
        P(),
        P(),
    )
    out_specs = (P("user", "seq", None), P(("user", "seq"), None))
    return jax.shard_map(body, mesh=mesh, in_specs=in_specs, out_specs=out_specs, check_vma=False)
```

time: 293 us -> 89.6 us (0.31)
  the two profiles are of different devices: /device:TPU:1 before, /device:TPU:8 now
where the time goes in v1:
time: 89.6 us; the launch traced here: 89.2 us
  Pallas kernels  79.5 us (89%)
  local copies, waits for them, and re-layouts  8.44 us (9%)
  between operations  1.3 us (1%)
    pallas_call x1, Pallas kernels, body(): pl.pallas_call(kernel, out_shape=(jax.ShapeDtypeStruct((HR, D), BF16), ja...  79.5 us
    unnamed x18, local copies, waits for them, and re-layouts  8.44 us

profile of v1, /device:TPU:8, one launch (start us, length us, event | category | flops | bytes accessed | tf_op | source)
XLA Modules:
  0.0 89.2 jit_solution(7259708008781256613)
XLA Ops:
  1.3 0.0 copy-start
  1.3 1.6 %copy-done = bf16[1024,1024]{1,0:T(8,128)(2,1)S(1)} copy-done((bf16[1024,1024]{1,0:T(8,128)(2,1)S(1)}, bf16[1024,1024]{1,0:T(8,128)(2,1)}, u32[]{:S(2)}) %copy-start) | copy-done | bytes 2097176
  2.9 0.0 copy-start.1
  2.9 1.0 %copy-done.1 = bf16[1024,1,256]{2,0,1:T(8,128)(2,1)S(1)} copy-done((bf16[1024,1,256]{2,0,1:T(8,128)(2,1)S(1)}, bf16[1024,1,256]{2,0,1:T(8,128)(2,1)}, u32[]{:S(2)}) %copy-start.1) | copy-done | bytes 524312
  3.9 0.0 copy-start.2
  3.9 0.9 %copy-done.2 = bf16[1,128,1024]{2,1,0:T(8,128)(2,1)S(1)} copy-done((bf16[1,128,1024]{2,1,0:T(8,128)(2,1)S(1)}, bf16[1,128,1024]{2,1,0:T(8,128)(2,1)}, u32[]{:S(2)}) %copy-start.2) | copy-done | bytes 262168
  4.9 0.0 copy-start.3
  4.9 0.8 copy-done.3
  5.7 0.0 copy-start.4
  5.7 0.7 copy-done.4
  6.4 0.0 copy-start.5
  6.4 0.7 copy-done.5
  7.1 0.0 copy-start.6
  7.1 0.7 copy-done.6
  7.7 0.0 copy-start.7
  7.7 0.7 copy-done.7
  8.4 79.5 %shard_map.104 = (bf16[128,1024]{1,0:T(8,128)(2,1)S(1)}, bf16[32,1024]{1,0:T(8,128)(2,1)S(1)}) custom-call(bf16[128,1024]{1,0:T(8,128)(2,1)S(1)} %bitcast.7, s32[1]{0:T(128)S(6)} %copy.13.length_in, s32[1,128]{1,0:T(1,128)S(1)} %copy-done.6, bf16[32,1024]{1,0:T(8,128)(2,1)S(1)} %copy-done.3, s32[1,32]{1,0:T(1,128)S(1)} %bitcast.9, ...), custom_call_target="tpu_custom_call" | custom-call | flops 4000000000 | bytes 8000000 | tf_op jit(solution)/shard_map/pallas_call | solution.py:580
  87.9 0.7 copy.14
  88.6 0.6 copy.15
Async XLA Ops:
  1.3 1.6 %copy-start = (bf16[1024,1024]{1,0:T(8,128)(2,1)S(1)}, bf16[1024,1024]{1,0:T(8,128)(2,1)}, u32[]{:S(2)}) copy-start(bf16[1024,1024]{1,0:T(8,128)(2,1)} %out_w_in.1) | copy-start | bytes 6291460
  2.9 1.0 %copy-start.1 = (bf16[1024,1,256]{2,0,1:T(8,128)(2,1)S(1)}, bf16[1024,1,256]{2,0,1:T(8,128)(2,1)}, u32[]{:S(2)}) copy-start(bf16[1024,1,256]{2,0,1:T(8,128)(2,1)} %param.14) | copy-start | bytes 1572868
  3.9 0.9 %copy-start.2 = (bf16[1,128,1024]{2,1,0:T(8,128)(2,1)S(1)}, bf16[1,128,1024]{2,1,0:T(8,128)(2,1)}, u32[]{:S(2)}) copy-start(bf16[1,128,1024]{2,1,0:T(8,128)(2,1)} %param.9) | copy-start | bytes 786436
  4.9 0.8 copy-start.3
  5.7 0.7 copy-start.4
  6.4 0.7 copy-start.5
  7.1 0.7 copy-start.6
  7.7 0.7 copy-start.7

commit v2 on v1

v2 whole, which is shorter than its diff:
```python
import functools

import jax
import jax.numpy as jnp
from jax import lax
from jax.experimental import pallas as pl
from jax.experimental.pallas import tpu as pltpu
from jax.sharding import PartitionSpec as P

MESH = pl.DeviceIdType.MESH
NORM_EPS = 1e-05
NX, NZ, NY = 4, 8, 8
NU, NS = NX * NZ, NY * 2
D = 1024
DH = 64
NB = 32
HR = 128
CR = 64
HIST = HR * NS
PAY_V = 2 * HR
PAY_Q = 3 * HR
PAY_B = 3 * HR + CR
PAY = PAY_B + 16
F32 = jnp.float32
BF16 = jnp.bfloat16


def dot(a, b):
    return jnp.dot(a, b, preferred_element_type=F32)


def dot_nt(a, b):
    return lax.dot_general(a, b, (((1,), (1,)), ((), ())), preferred_element_type=F32)


def iota(shape, axis):
    return lax.broadcasted_iota(jnp.int32, shape, axis)


def half_silu(h):
    return h * jnp.tanh(h) + h


def swap(a):
    return pltpu.roll(a, DH, axis=1)


def low_lanes(rows):
    return iota((rows, 128), 1) < DH


def join(lo, hi):
    return jnp.where(low_lanes(lo.shape[0]), lo, swap(hi))


def kernel(
    hist_in,
    length_hbm,
    bucket_hbm,
    cand_hbm,
    owner_hbm,
    weight_in,
    bias_hbm,
    gain_hbm,
    out_w_in,
    hist_out,
    cand_out,
    length_in,
    bucket_in,
    cand_in,
    owner_in,
    bias_in,
    gain_in,
    feats,
    weights,
    out_w,
    bucket_own,
    bucket_sib,
    cand_send,
    cand_arr,
    pay,
    got,
    gate_own,
    gate_send,
    gate_sib,
    wide,
    queries,
    keys,
    values,
    acc,
    back_c,
    back_h,
    arr_c,
    arr_h,
    done_send,
    done_arr,
    local_sem,
    ring_s,
    ring_r,
    side_s,
    side_r,
    far_s,
    far_r,
    cand_s,
    cand_r,
    pay_s,
    pay_r,
    sib_s,
    sib_r,
    back_cs,
    back_cr,
    back_hs,
    back_hr,
    done_s,
    done_r,
):
    user = lax.axis_index("user")
    seq = lax.axis_index("seq")
    x, z = user // NZ, user % NZ
    y, core = seq // 2, seq % 2
    part = (x + z) % 4
    sibling = (user, y * 2 + (1 - core))

    def along_y(step):
        return (user, ((y + NY + step) % NY) * 2 + core)

    def along_x(step):
        return (((x + NX + step) % NX) * NZ + z, seq)

    def along_z(step):
        return (x * NZ + (z + NZ + step) % NZ, seq)

    def remote(src, dst, send, recv, to):
        return pltpu.make_async_remote_copy(
            src_ref=src, dst_ref=dst, send_sem=send, recv_sem=recv, device_id=to, device_id_type=MESH
        )

    barrier = pltpu.get_barrier_semaphore()

    def greet_user(t, carry):
        pl.semaphore_signal(barrier, inc=1, device_id=((user + t) % NU, seq), device_id_type=MESH)
        return carry

    def greet_seq(t, carry):
        pl.semaphore_signal(barrier, inc=1, device_id=(user, (seq + t) % NS), device_id_type=MESH)
        return carry

    lax.fori_loop(1, NU, greet_user, 0)
    lax.fori_loop(1, NS, greet_seq, 0)

    own_weight = pltpu.make_async_copy(weight_in, weights.at[y], local_sem.at[0])
    own_feats = pltpu.make_async_copy(hist_in, feats.at[pl.ds(0, HR)], local_sem.at[1])
    own_out_w = pltpu.make_async_copy(out_w_in, out_w, local_sem.at[2])
    small = [
        pltpu.make_async_copy(src, dst, local_sem.at[6 + n])
        for n, (src, dst) in enumerate(
            (
                (owner_hbm, owner_in),
                (cand_hbm, cand_in),
                (bucket_hbm, bucket_in),
                (length_hbm, length_in),
                (bias_hbm, bias_in),
                (gain_hbm, gain_in),
            )
        )
    ]
    for copy in small:
        copy.start()
    own_weight.start()
    own_feats.start()
    own_out_w.start()

    pl.semaphore_wait(barrier, NU - 1 + NS - 1)

    sent = []

    def go(copy):
        copy.start()
        sent.append(copy)

    def quarter(origin, cls, half, at=0, rows=128):
        start = pl.multiple_of(cls * 256 + half * 128 + at, 64)
        return weights.at[origin, pl.ds(start, rows)]

    def ring_copy(dirn, step, half, src):
        sign = 1 if dirn == 0 else -1
        origin = (y + NY - sign * (step - 1)) % NY
        dst = quarter(origin, part, half)
        return remote(
            dst if src is None else src,
            dst,
            ring_s.at[dirn, step - 1, half],
            ring_r.at[dirn, step - 1, half],
            along_y(sign),
        )

    for half in range(2):
        start = pl.multiple_of(part * 256 + half * 128, 128)
        for dirn in range(2):
            go(ring_copy(dirn, 1, half, weight_in.at[pl.ds(start, 128)]))
    go(remote(hist_in, feats.at[pl.ds(HR, HR)], sib_s.at[0], sib_r.at[0], sibling))

    for copy in small:
        copy.wait()
    lane = iota((32, 128), 1)
    row = iota((32, 128), 0)
    owner_row = jnp.concatenate([owner_in[...].astype(F32), jnp.zeros((1, 96), F32)], axis=1)
    owner_wide = jnp.broadcast_to(owner_row, (32, 128))
    owner_col = jnp.sum(jnp.where(lane == row, owner_wide, 0.0), axis=1, keepdims=True)
    same = (owner_wide == owner_col) & (lane < 32)
    rank_row = jnp.sum(jnp.where(same & (row < lane), 1.0, 0.0), axis=0, keepdims=True)
    rank_col = jnp.sum(jnp.where(same & (lane < row), 1.0, 0.0), axis=1, keepdims=True)
    slot_row = owner_row * 2.0 + rank_row
    slot_col = owner_col * 2.0 + rank_col

    def split_rows(slots, out):
        for k in range(8):
            wide[pl.ds(k, CR, stride=8), :] = slots[:, 128 * k : 128 * k + 128]
        out[...] = wide[...].astype(BF16)

    def join_rows(arrived):
        wide[...] = arrived[...].astype(F32)
        return [wide[pl.ds(k, CR, stride=8), :].astype(BF16) for k in range(8)]

    put = jnp.where(iota((CR, 32), 0).astype(F32) == slot_row[:, 0:32], 1.0, 0.0).astype(BF16)
    split_rows(dot(put, cand_in[...]), cand_send)
    bucket_own[...] = jnp.broadcast_to(bucket_in[...].astype(F32), (16, 128)).astype(BF16)
    go(remote(bucket_own, bucket_sib, sib_s.at[1], sib_r.at[1], sibling))

    def cand_copy(t):
        to = (user + t) % NU
        return remote(
            cand_send.at[pl.ds(pl.multiple_of(to * 16, 16), 16)],
            cand_arr.at[pl.ds(pl.multiple_of(user * 16, 16), 16)],
            cand_s.at[t],
            cand_r.at[t],
            (to, seq),
        )

    def cand_start(t, carry):
        cand_copy(t).start()
        return carry

    lax.fori_loop(1, NU, cand_start, 0)
    mine = pl.ds(pl.multiple_of(user * 16, 16), 16)
    own_cand = pltpu.make_async_copy(cand_send.at[mine], cand_arr.at[mine], local_sem.at[3])
    own_cand.start()

    def origin_of(dirn, step):
        sign = 1 if dirn == 0 else -1
        return (y + NY - sign * step) % NY

    def index_of(dirn, step):
        return 2 * (step - 1) + (dirn if step < 4 else 0)

    def side_copy(dirn, step, half, way):
        ref = quarter(origin_of(dirn, step), part, half)
        o = index_of(dirn, step)
        to = along_x(1 if way == 0 else -1)
        return remote(ref, ref, side_s.at[o, half, way], side_r.at[o, half, way], to)

    def far_copy(dirn, step, half):
        ref = quarter(origin_of(dirn, step), part, half)
        o = index_of(dirn, step)
        to = along_z(2 if half == 0 else -2)
        return remote(ref, ref, far_s.at[o, half], far_r.at[o, half], to)

    def ring_step(step):
        for half in range(2):
            for dirn in range(2):
                if step == 4 and dirn != half:
                    continue
                ring_copy(dirn, step, half, None).wait_recv()
                if step < 3 or (step == 3 and dirn == half):
                    go(ring_copy(dirn, step + 1, half, None))
                for way in range(2):
                    go(side_copy(dirn, step, half, way))
                go(far_copy(dirn, step, half))

    def side_step(step):
        for half in range(2):
            for dirn in range(2 if step < 4 else 1):
                for way in range(2):
                    side_copy(dirn, step, half, way).wait_recv()
                far_copy(dirn, step, half).wait_recv()

    is_first = core == 0

    def project(origin, slot):
        acc = dot(feats[...], weights[origin])
        full = half_silu(acc * 0.5)
        gv, qk = full[:, 0:128], full[:, 128:256]
        gvb = gv.astype(BF16)
        gate_own[origin, 0:HR] = gvb[0:HR]
        gate_own[origin, HR : HR + CR] = gvb[2 * HR : 2 * HR + CR]
        gate_send[origin, 0:HR] = gvb[HR : 2 * HR]
        gate_send[origin, HR : HR + CR] = gvb[2 * HR + CR : 2 * HR + 2 * CR]
        at_own = pl.multiple_of(core * HR, HR)
        at_sib = pl.multiple_of((1 - core) * HR, HR)
        pay[slot, pl.ds(at_own, HR)] = qk[0:HR].astype(BF16)
        pay[slot, pl.ds(at_sib, HR)] = qk[HR : 2 * HR].astype(BF16)
        low = low_lanes(HR)
        own_v, sib_v = gv[0:HR], gv[HR : 2 * HR]
        v_pair = jnp.where(
            is_first, jnp.where(low, swap(own_v), sib_v), jnp.where(low, swap(sib_v), own_v)
        )
        pay[slot, PAY_V : PAY_V + HR] = v_pair.astype(BF16)
        own_q, sib_q = qk[2 * HR : 2 * HR + CR], qk[2 * HR + CR : 2 * HR + 2 * CR]
        q_pair = jnp.where(is_first, join(own_q, sib_q), join(sib_q, own_q))
        pay[slot, PAY_Q : PAY_Q + CR] = q_pair.astype(BF16)
        first = iota((16, 128), 0) == core
        pay[slot, PAY_B : PAY_B + 16] = jnp.where(
            first, bucket_own[...].astype(F32), bucket_sib[...].astype(F32)
        ).astype(BF16)

    def pay_copy(rel):
        to = (y + rel + NY // 2) % NY
        return remote(pay.at[rel], got.at[y], pay_s.at[rel], pay_r.at[rel], (user, to * 2 + core))

    def project_step(step):
        def one(k, carry):
            rel = jnp.where(k == 0, step, NY - step)
            project((y + rel) % NY, rel)
            pay_copy(rel).start()
            return carry

        lax.fori_loop(0, 2, one, 0)

    ring_step(1)

    def cand_wait(t, carry):
        cand_copy(t).wait_recv()
        return carry

    lax.fori_loop(1, NU, cand_wait, 0)
    own_cand.wait()
    for k, columns in enumerate(join_rows(cand_arr)):
        feats[2 * HR : 2 * HR + CR, 128 * k : 128 * k + 128] = columns
    go(
        remote(
            feats.at[pl.ds(2 * HR, CR)],
            feats.at[pl.ds(2 * HR + CR, CR)],
            sib_s.at[2],
            sib_r.at[2],
            sibling,
        )
    )
    ring_step(2)

    own_feats.wait()
    own_weight.wait()
    remote(hist_in, feats.at[pl.ds(HR, HR)], sib_s.at[0], sib_r.at[0], sibling).wait_recv()
    remote(bucket_own, bucket_sib, sib_s.at[1], sib_r.at[1], sibling).wait_recv()
    remote(
        feats.at[pl.ds(2 * HR, CR)],
        feats.at[pl.ds(2 * HR + CR, CR)],
        sib_s.at[2],
        sib_r.at[2],
        sibling,
    ).wait_recv()
    project(y, 0)
    pay_copy(0).start()
    head_sel = iota((16, 128), 0) == 2 * ((y + NY // 2) % NY) + core
    table = jnp.concatenate([bias_in[...], jnp.zeros((16, 96), F32)], axis=1) * 0.5
    bias_row = jnp.sum(jnp.where(head_sel, table, 0.0), axis=0, keepdims=True)
    bias_hi = bias_row.astype(BF16).astype(F32)
    bias_lo = bias_row - bias_hi
    bias_lanes = pltpu.roll(jnp.broadcast_to(bias_hi, (8, 128)), DH, axis=1) + pltpu.roll(
        jnp.broadcast_to(bias_lo, (8, 128)), DH + NB, axis=1
    )
    bias_lanes = bias_lanes[0:1]
    length = length_in[0]

    low = low_lanes(HR)
    lane_h = iota((HR, 128), 1)
    row_h = iota((HR, 128), 0)

    def prepare(src):
        v_pair = got[src, PAY_V : PAY_V + HR].astype(F32)
        v_swap = swap(v_pair)
        buckets = got[src, PAY_B : PAY_B + 16].astype(F32)
        base = src * (2 * HR)
        for c in range(2):
            qk = got[src, c * HR : c * HR + HR].astype(F32)
            at = c * HR
            queries[src, at : at + HR] = jnp.where(low, qk * 0.0625, bias_lanes).astype(BF16)
            mine_b = jnp.sum(jnp.where(lane_h == row_h, buckets[c : c + 1], 0.0), axis=1, keepdims=True)
            hit = jnp.where((lane_h & (NB - 1)).astype(F32) == mine_b, 1.0, 0.0)
            keys[src, at : at + HR] = jnp.where(low, swap(qk), hit).astype(BF16)
            v = jnp.where(low, v_pair, v_swap) if c == 0 else jnp.where(low, v_swap, v_pair)
            values[src, at : at + HR] = jnp.where(row_h + (base + at) < length, v, 0.0).astype(BF16)
        q_pair = got[src, PAY_Q : PAY_Q + CR].astype(F32)
        low_c = low_lanes(CR)
        at = 2 * HR
        queries[src, at : at + CR] = jnp.where(low_c, q_pair * 0.0625, bias_lanes).astype(BF16)
        queries[src, at + CR : at + 2 * CR] = jnp.where(low_c, swap(q_pair) * 0.0625, bias_lanes).astype(BF16)

    def source(m):
        return (y + NY // 2 + jnp.where(m % 2 == 1, (m + 1) // 2, NY - m // 2)) % NY

    def weigh(q, src, mask=None):
        w = half_silu(dot_nt(q, keys[src]))
        if mask is not None:
            w = jnp.where(mask, w, 0.0)
        return dot(w.astype(BF16), values[src])

    def take_in(*new):
        for m in new:
            prepare(source(m))
        tri = iota((2 * HR + 2 * CR, 2 * HR), 1) <= iota((2 * HR + 2 * CR, 2 * HR), 0)
        own = [source(m) for m in new]
        for n, part_sum in [(n, weigh(queries[n], n, tri)) for n in own]:
            acc[n] = part_sum
        pairs = [(source(m), source(k)) for m in new for k in range(m)]
        for at in range(0, len(pairs), 4):
            sums = []
            for n, a in pairs[at : at + 4]:
                later, earlier = jnp.where(a < n, n, a), jnp.where(a < n, a, n)
                sums.append((later, 0, weigh(queries[later], earlier)))
                sums.append((earlier, 2 * HR, weigh(queries[earlier, 2 * HR :], later)))
            for src, first, part_sum in sums:
                acc[src, first:] += part_sum

    def take_in_step(step):
        pay_copy(NY - step).wait_recv()
        pay_copy(step).wait_recv()
        take_in(2 * step - 1, 2 * step)

    def back_c_copy(to):
        return remote(
            back_c.at[to], arr_c.at[seq], back_cs.at[to], back_cr.at[seq], (user, to)
        )

    def back_h_copy(to):
        return remote(
            back_h.at[to], arr_h.at[seq], back_hs.at[to], back_hr.at[seq], (user, to)
        )

    def send_back(to, copy, out, arr):
        @pl.when(to != seq)
        def _():
            copy(to).start()

        @pl.when(to == seq)
        def _():
            arr[seq] = out

    def send_cands(i, carry):
        for c in range(2):
            at = 2 * HR + c * CR
            lo, hi = acc[i, at : at + CR // 2], acc[i, at + CR // 2 : at + CR]
            packed = jnp.where(low_lanes(CR // 2), lo, hi).astype(BF16)
            to = i * 2 + c
            back_c[to] = packed
            send_back(to, back_c_copy, packed, arr_c)
        return carry

    def send_hist(i, carry):
        for c in range(2):
            at = c * HR
            lo, hi = acc[i, at : at + HR // 2], acc[i, at + HR // 2 : at + HR]
            packed = jnp.where(low_lanes(HR // 2), lo, hi).astype(BF16)
            to = i * 2 + c
            back_h[to] = packed
            send_back(to, back_h_copy, packed, arr_h)
        return carry

    side_step(1)
    project_step(1)
    ring_step(3)
    side_step(2)
    project_step(2)
    ring_step(4)
    side_step(3)
    project_step(3)
    pay_copy(0).wait_recv()
    take_in(0)
    take_in_step(1)
    side_step(4)
    project((y + 4) % NY, 4)
    own_pay = pltpu.make_async_copy(pay.at[4], got.at[y], local_sem.at[4])
    own_pay.start()
    gate_copy = remote(gate_send, gate_sib, sib_s.at[3], sib_r.at[3], sibling)
    go(gate_copy)
    take_in_step(2)
    take_in_step(3)
    last = source(7)
    lax.fori_loop(0, last, send_hist, 0)
    own_pay.wait()
    take_in(7)
    lax.fori_loop(0, NY, send_cands, 0)
    lax.fori_loop(last, NY, send_hist, 0)

    def wait_back(copy_sem, arr, back):
        def one(t, carry):
            src = (seq + t) % NS
            remote(back.at[src], arr.at[src], copy_sem[0].at[src], copy_sem[1].at[src], (user, src)).wait_recv()
            return carry

        lax.fori_loop(1, NS, one, 0)

    def finish(arr, rows, at, inputs):
        half = rows // 2
        low_half, low_rows = low_lanes(half), low_lanes(rows)
        tiles, total = [], jnp.zeros((rows, 128), F32)
        for p in range(NY):
            at_p = 2 * ((p + NY // 2) % NY)
            even, odd = arr[at_p].astype(F32), arr[at_p + 1].astype(F32)
            tile = jnp.concatenate(
                [jnp.where(low_half, even, swap(odd)), jnp.where(low_half, swap(even), odd)], axis=0
            )
            tiles.append(tile)
            total = total + tile
        mean = jnp.sum(total, axis=1, keepdims=True) * (1.0 / D)
        tiles = [t - mean for t in tiles]
        squares = jnp.zeros((rows, 128), F32)
        for t in tiles:
            squares = squares + t * t
        var = jnp.sum(squares, axis=1, keepdims=True) * (1.0 / D)
        scale = lax.rsqrt(var + NORM_EPS)
        gated = []
        for p in range(NY):
            own = gate_own[p, at : at + rows].astype(F32)
            sib = gate_sib[p, at : at + rows].astype(F32)
            even, odd = jnp.where(is_first, own, sib), jnp.where(is_first, sib, own)
            gate = jnp.where(low_rows, even, swap(odd))
            g = tiles[p] * scale * gain_in[:, 128 * p : 128 * p + 128] * gate
            gated.append(g.astype(BF16))
        result = dot(jnp.concatenate(gated, axis=1), out_w[...])
        return result + inputs.astype(F32)

    gate_copy.wait_recv()
    own_out_w.wait()
    wait_back((back_cs, back_cr), arr_c, back_c)
    cand_done = finish(arr_c, CR, HR, feats[2 * HR : 2 * HR + CR])
    split_rows(cand_done, done_send)

    def done_copy(t):
        to = (user + t) % NU
        return remote(
            done_send.at[pl.ds(pl.multiple_of(to * 16, 16), 16)],
            done_arr.at[pl.ds(pl.multiple_of(user * 16, 16), 16)],
            done_s.at[t],
            done_r.at[t],
            (to, seq),
        )

    def done_start(t, carry):
        done_copy(t).start()
        return carry

    lax.fori_loop(1, NU, done_start, 0)
    own_done = pltpu.make_async_copy(done_send.at[mine], done_arr.at[mine], local_sem.at[5])
    own_done.start()

    wait_back((back_hs, back_hr), arr_h, back_h)
    hist_out[...] = finish(arr_h, HR, 0, feats[0:HR]).astype(BF16)

    def done_wait(t, carry):
        done_copy(t).wait_recv()
        return carry

    lax.fori_loop(1, NU, done_wait, 0)
    own_done.wait()
    pick = jnp.where(iota((32, CR), 1).astype(F32) == slot_col, 1.0, 0.0).astype(BF16)
    for k, columns in enumerate(join_rows(done_arr)):
        cand_out[:, 128 * k : 128 * k + 128] = dot(pick, columns).astype(BF16)

    for copy in sent:
        copy.wait_send()

    def user_sends(t, carry):
        cand_copy(t).wait_send()
        done_copy(t).wait_send()
        return carry

    def pay_sends(t, carry):
        pay_copy((t + 4) % NY).wait_send()
        return carry

    def back_sends(t, carry):
        to = (seq + t) % NS
        back_c_copy(to).wait_send()
        back_h_copy(to).wait_send()
        return carry

    lax.fori_loop(1, NU, user_sends, 0)
    lax.fori_loop(1, NY, pay_sends, 0)
    lax.fori_loop(1, NS, back_sends, 0)


def body(hist, length, bucket, cand, owner, weight, bias, gain, out_weight):
    vmem = pl.BlockSpec(memory_space=pltpu.VMEM)
    hbm = pl.BlockSpec(memory_space=pltpu.HBM)
    dma = pltpu.SemaphoreType.DMA
    hist_out, cand_out = pl.pallas_call(
        kernel,
        out_shape=(
            jax.ShapeDtypeStruct((HR, D), BF16),
            jax.ShapeDtypeStruct((32, D), BF16),
        ),
        in_specs=[hbm] * 9,
        out_specs=(vmem, vmem),
        scratch_shapes=[
            pltpu.SMEM((1,), jnp.int32),
            pltpu.VMEM((1, 128), jnp.int32),
            pltpu.VMEM((32, D), BF16),
            pltpu.VMEM((1, 32), jnp.int32),
            pltpu.VMEM((NS, NB), F32),
            pltpu.VMEM((1, D), F32),
            pltpu.VMEM((2 * HR + 2 * CR, D), BF16),
            pltpu.VMEM((NY, D, 4 * DH), BF16),
            pltpu.VMEM((D, D), BF16),
            pltpu.VMEM((16, 128), BF16),
            pltpu.VMEM((16, 128), BF16),
            pltpu.VMEM((512, 128), BF16),
            pltpu.VMEM((512, 128), BF16),
            pltpu.VMEM((NY, PAY, 128), BF16),
            pltpu.VMEM((NY, PAY, 128), BF16),
            pltpu.VMEM((NY, HR + CR, 128), BF16),
            pltpu.VMEM((NY, HR + CR, 128), BF16),
            pltpu.VMEM((NY, HR + CR, 128), BF16),
            pltpu.VMEM((512, 128), F32),
            pltpu.VMEM((NY, 2 * HR + 2 * CR, 128), BF16),
            pltpu.VMEM((NY, 2 * HR, 128), BF16),
            pltpu.VMEM((NY, 2 * HR, 128), BF16),
            pltpu.VMEM((NY, 2 * HR + 2 * CR, 128), F32),
            pltpu.VMEM((NS, CR // 2, 128), BF16),
            pltpu.VMEM((NS, HR // 2, 128), BF16),
            pltpu.VMEM((NS, CR // 2, 128), BF16),
            pltpu.VMEM((NS, HR // 2, 128), BF16),
            pltpu.VMEM((512, 128), BF16),
            pltpu.VMEM((512, 128), BF16),
            dma((12,)),
            dma((2, 4, 2)),
            dma((2, 4, 2)),
            dma((7, 2, 2)),
            dma((7, 2, 2)),
            dma((7, 2)),
            dma((7, 2)),
            dma((NU,)),
            dma((NU,)),
            dma((NY,)),
            dma((NY,)),
            dma((4,)),
            dma((4,)),
            dma((NS,)),
            dma((NS,)),
            dma((NS,)),
            dma((NS,)),
            dma((NU,)),
            dma((NU,)),
        ],
        compiler_params=pltpu.CompilerParams(
            collective_id=0, has_side_effects=True, vmem_limit_bytes=60 * 1024 * 1024
        ),
        cost_estimate=pl.CostEstimate(
            flops=4 * 10**9, bytes_accessed=8 * 10**6, transcendentals=5 * 10**6
        ),
    )(
        hist.reshape(HR, D),
        length,
        bucket,
        cand,
        owner.reshape(1, 32),
        weight.reshape(D, 4 * DH),
        bias,
        gain.reshape(1, D),
        out_weight,
    )
    return hist_out.reshape(1, HR, D), cand_out


def solution(mesh):
    in_specs = (
        P("user", "seq", None),
        P("user"),
        P("user", "seq"),
        P(("user", "seq"), None),
        P(("user", "seq"), None),
        P(None, "seq", None),
        P(),
        P(),
        P(),
    )
    out_specs = (P("user", "seq", None), P(("user", "seq"), None))
    return jax.shard_map(body, mesh=mesh, in_specs=in_specs, out_specs=out_specs, check_vma=False)
```

time: 89.6 us -> 80.1 us (0.89)
  the two profiles are of different devices: /device:TPU:8 before, /device:TPU:1 now
where the time goes in v2:
time: 80.1 us; the launch traced here: 79 us
  Pallas kernels  74.5 us (93%)
  local copies, waits for them, and re-layouts  3.14 us (4%)
  between operations  1.29 us (2%)
    pallas_call x1, Pallas kernels, body(): pl.pallas_call(kernel, out_shape=(jax.ShapeDtypeStruct((HR, D), BF16), ja...  74.5 us
    unnamed x2, local copies, waits for them, and re-layouts  3.14 us

profile of v2, /device:TPU:1, one launch (start us, length us, event | category | flops | bytes accessed | tf_op | source)
XLA Modules:
  0.0 79.0 jit_solution(14885327623744858813)
XLA Ops:
  1.3 74.5 %shard_map.104 = (bf16[128,1024]{1,0:T(8,128)(2,1)}, bf16[32,1024]{1,0:T(8,128)(2,1)}) custom-call(bf16[128,1024]{1,0:T(8,128)(2,1)} %bitcast.7, s32[1]{0:T(128)S(6)} %copy.13.length_hbm, s32[1,128]{1,0:T(1,128)} %bucket_hbm.1, bf16[32,1024]{1,0:T(8,128)(2,1)} %cand_hbm.1, s32[1,32]{1,0:T(1,128)} %bitcast.9, bf16[1024,256]{1,0:T(8,128)(2,1)} %bitcast.6, ...), custom_call_target="tpu_custom_call" | custom-call | flops 4000000000 | bytes 8000000 | tf_op jit(solution)/shard_map/pallas_call | solution.py:596
  75.8 1.7 %copy.14 = bf16[1,128,1024]{2,1,0:T(8,128)(2,1)} copy(bf16[1,128,1024]{2,1,0:T(8,128)(2,1)} %bitcast.5) | data formatting | bytes 524288
  77.5 1.5 %copy.15 = bf16[32,1024]{1,0:T(8,128)(2,1)} copy(bf16[32,1024]{1,0:T(8,128)(2,1)} %get-tuple-element.9) | data formatting | bytes 131072

commit v3 on v2

--- a/solution.py
+++ b/solution.py
@@ -18,9 +18,9 @@
 CR = 64
 HIST = HR * NS
 PAY_V = 2 * HR
-PAY_Q = 3 * HR
-PAY_B = 3 * HR + CR
-PAY = PAY_B + 16
+PAY_B = 3 * HR
+PAY_Q = PAY_B + 16
+PAY = PAY_Q + CR
 F32 = jnp.float32
 BF16 = jnp.bfloat16
 
@@ -65,6 +65,8 @@
     out_w_in,
     hist_out,
     cand_out,
+    hist_done,
+    gain_gate,
     length_in,
     bucket_in,
     cand_in,
@@ -170,36 +172,6 @@
     own_feats.start()
     own_out_w.start()
 
-    pl.semaphore_wait(barrier, NU - 1 + NS - 1)
-
-    sent = []
-
-    def go(copy):
-        copy.start()
-        sent.append(copy)
-
-    def quarter(origin, cls, half, at=0, rows=128):
-        start = pl.multiple_of(cls * 256 + half * 128 + at, 64)
-        return weights.at[origin, pl.ds(start, rows)]
-
-    def ring_copy(dirn, step, half, src):
-        sign = 1 if dirn == 0 else -1
-        origin = (y + NY - sign * (step - 1)) % NY
-        dst = quarter(origin, part, half)
-        return remote(
-            dst if src is None else src,
-            dst,
-            ring_s.at[dirn, step - 1, half],
-            ring_r.at[dirn, step - 1, half],
-            along_y(sign),
-        )
-
-    for half in range(2):
-        start = pl.multiple_of(part * 256 + half * 128, 128)
-        for dirn in range(2):
-            go(ring_copy(dirn, 1, half, weight_in.at[pl.ds(start, 128)]))
-    go(remote(hist_in, feats.at[pl.ds(HR, HR)], sib_s.at[0], sib_r.at[0], sibling))
-
     for copy in small:
         copy.wait()
     lane = iota((32, 128), 1)
@@ -225,6 +197,37 @@
     put = jnp.where(iota((CR, 32), 0).astype(F32) == slot_row[:, 0:32], 1.0, 0.0).astype(BF16)
     split_rows(dot(put, cand_in[...]), cand_send)
     bucket_own[...] = jnp.broadcast_to(bucket_in[...].astype(F32), (16, 128)).astype(BF16)
+
+    pl.semaphore_wait(barrier, NU - 1 + NS - 1)
+
+    sent = []
+
+    def go(copy):
+        copy.start()
+        sent.append(copy)
+
+    def quarter(origin, cls, half, at=0, rows=128):
+        start = pl.multiple_of(cls * 256 + half * 128 + at, 64)
+        return weights.at[origin, pl.ds(start, rows)]
+
+    def ring_copy(dirn, step, piece, src):
+        sign = 1 if dirn == 0 else -1
+        origin = (y + NY - sign * (step - 1)) % NY
+        dst = quarter(origin, part, piece // 2, 64 * (piece % 2), 64)
+        return remote(
+            dst if src is None else src,
+            dst,
+            ring_s.at[dirn, step - 1, piece],
+            ring_r.at[dirn, step - 1, piece],
+            along_y(sign),
+        )
+
+    for piece in range(4):
+        start = pl.multiple_of(part * 256 + piece * 64, 64)
+        for dirn in range(2):
+            go(ring_copy(dirn, 1, piece, weight_in.at[pl.ds(start, 64)]))
+    go(remote(hist_in, feats.at[pl.ds(HR, HR)], sib_s.at[0], sib_r.at[0], sibling))
+
     go(remote(bucket_own, bucket_sib, sib_s.at[1], sib_r.at[1], sibling))
 
     def cand_copy(t):
@@ -270,9 +273,10 @@
             for dirn in range(2):
                 if step == 4 and dirn != half:
                     continue
-                ring_copy(dirn, step, half, None).wait_recv()
-                if step < 3 or (step == 3 and dirn == half):
-                    go(ring_copy(dirn, step + 1, half, None))
+                for piece in (2 * half, 2 * half + 1):
+                    ring_copy(dirn, step, piece, None).wait_recv()
+                    if step < 3 or (step == 3 and dirn == half):
+                        go(ring_copy(dirn, step + 1, piece, None))
                 for way in range(2):
                     go(side_copy(dirn, step, half, way))
                 go(far_copy(dirn, step, half))
@@ -286,15 +290,18 @@
 
     is_first = core == 0
 
-    def project(origin, slot):
-        acc = dot(feats[...], weights[origin])
-        full = half_silu(acc * 0.5)
+    def project(*heads):
+        sums = [dot(feats[...], weights[origin]) for origin, slot in heads]
+        for (origin, slot), part_sum in zip(heads, sums):
+            full = half_silu(part_sum * 0.5)
+            pack_hist(origin, slot, full[0 : 2 * HR])
+            pack_cand(origin, slot, full[2 * HR :])
+
+    def pack_hist(origin, slot, full):
         gv, qk = full[:, 0:128], full[:, 128:256]
         gvb = gv.astype(BF16)
         gate_own[origin, 0:HR] = gvb[0:HR]
-        gate_own[origin, HR : HR + CR] = gvb[2 * HR : 2 * HR + CR]
         gate_send[origin, 0:HR] = gvb[HR : 2 * HR]
-        gate_send[origin, HR : HR + CR] = gvb[2 * HR + CR : 2 * HR + 2 * CR]
         at_own = pl.multiple_of(core * HR, HR)
         at_sib = pl.multiple_of((1 - core) * HR, HR)
         pay[slot, pl.ds(at_own, HR)] = qk[0:HR].astype(BF16)
@@ -305,28 +312,49 @@
             is_first, jnp.where(low, swap(own_v), sib_v), jnp.where(low, swap(sib_v), own_v)
         )
         pay[slot, PAY_V : PAY_V + HR] = v_pair.astype(BF16)
-        own_q, sib_q = qk[2 * HR : 2 * HR + CR], qk[2 * HR + CR : 2 * HR + 2 * CR]
-        q_pair = jnp.where(is_first, join(own_q, sib_q), join(sib_q, own_q))
-        pay[slot, PAY_Q : PAY_Q + CR] = q_pair.astype(BF16)
         first = iota((16, 128), 0) == core
         pay[slot, PAY_B : PAY_B + 16] = jnp.where(
             first, bucket_own[...].astype(F32), bucket_sib[...].astype(F32)
         ).astype(BF16)
 
+    def pack_cand(origin, slot, full):
+        gvb, qk = full[:, 0:128].astype(BF16), full[:, 128:256]
+        gate_own[origin, HR : HR + CR] = gvb[0:CR]
+        gate_send[origin, HR : HR + CR] = gvb[CR : 2 * CR]
+        own_q, sib_q = qk[0:CR], qk[CR : 2 * CR]
+        q_pair = jnp.where(is_first, join(own_q, sib_q), join(sib_q, own_q))
+        pay[slot, PAY_Q : PAY_Q + CR] = q_pair.astype(BF16)
+
     def pay_copy(rel):
         to = (y + rel + NY // 2) % NY
         return remote(pay.at[rel], got.at[y], pay_s.at[rel], pay_r.at[rel], (user, to * 2 + core))
 
+    def first_copy(at, rows, sem):
+        to = (y + NY // 2) % NY
+        return remote(
+            pay.at[0, pl.ds(at, rows)],
+            got.at[y, pl.ds(at, rows)],
+            pay_s.at[sem],
+            pay_r.at[sem],
+            (user, to * 2 + core),
+        )
+
+    first_hist = first_copy(0, PAY_Q, 0)
+    first_cand = first_copy(PAY_Q, CR, 4)
+
     def project_step(step):
-        def one(k, carry):
-            rel = jnp.where(k == 0, step, NY - step)
-            project((y + rel) % NY, rel)
-            pay_copy(rel).start()
-            return carry
-
-        lax.fori_loop(0, 2, one, 0)
-
+        project(((y + step) % NY, step), ((y + NY - step) % NY, NY - step))
+        pay_copy(step).start()
+        pay_copy(NY - step).start()
+
+    own_feats.wait()
+    own_weight.wait()
+    remote(hist_in, feats.at[pl.ds(HR, HR)], sib_s.at[0], sib_r.at[0], sibling).wait_recv()
+    remote(bucket_own, bucket_sib, sib_s.at[1], sib_r.at[1], sibling).wait_recv()
+    pack_hist(y, 0, half_silu(dot(feats[0 : 2 * HR], weights[y]) * 0.5))
+    first_hist.start()
     ring_step(1)
+    ring_step(2)
 
     def cand_wait(t, carry):
         cand_copy(t).wait_recv()
@@ -345,12 +373,6 @@
             sibling,
         )
     )
-    ring_step(2)
-
-    own_feats.wait()
-    own_weight.wait()
-    remote(hist_in, feats.at[pl.ds(HR, HR)], sib_s.at[0], sib_r.at[0], sibling).wait_recv()
-    remote(bucket_own, bucket_sib, sib_s.at[1], sib_r.at[1], sibling).wait_recv()
     remote(
         feats.at[pl.ds(2 * HR, CR)],
         feats.at[pl.ds(2 * HR + CR, CR)],
@@ -358,8 +380,8 @@
         sib_r.at[2],
         sibling,
     ).wait_recv()
-    project(y, 0)
-    pay_copy(0).start()
+    pack_cand(y, 0, half_silu(dot(feats[2 * HR :], weights[y]) * 0.5))
+    first_cand.start()
     head_sel = iota((16, 128), 0) == 2 * ((y + NY // 2) % NY) + core
     table = jnp.concatenate([bias_in[...], jnp.zeros((16, 96), F32)], axis=1) * 0.5
     bias_row = jnp.sum(jnp.where(head_sel, table, 0.0), axis=0, keepdims=True)
@@ -445,15 +467,19 @@
         def _():
             arr[seq] = out
 
-    def send_cands(i, carry):
-        for c in range(2):
-            at = 2 * HR + c * CR
-            lo, hi = acc[i, at : at + CR // 2], acc[i, at + CR // 2 : at + CR]
-            packed = jnp.where(low_lanes(CR // 2), lo, hi).astype(BF16)
-            to = i * 2 + c
-            back_c[to] = packed
-            send_back(to, back_c_copy, packed, arr_c)
-        return carry
+    def send_cands():
+        for off in (4, 3, 5, 2, 6, 1, 7, 0):
+            i = (y + off) % NY
+            for c in range(2):
+                at = 2 * HR + c * CR
+                lo, hi = acc[i, at : at + CR // 2], acc[i, at + CR // 2 : at + CR]
+                packed = jnp.where(low_lanes(CR // 2), lo, hi).astype(BF16)
+                to = i * 2 + c
+                back_c[to] = packed
+                if off:
+                    back_c_copy(to).start()
+                else:
+                    send_back(to, back_c_copy, packed, arr_c)
 
     def send_hist(i, carry):
         for c in range(2):
@@ -473,11 +499,12 @@
     ring_step(4)
     side_step(3)
     project_step(3)
-    pay_copy(0).wait_recv()
+    first_hist.wait_recv()
+    first_cand.wait_recv()
     take_in(0)
     take_in_step(1)
     side_step(4)
-    project((y + 4) % NY, 4)
+    project(((y + 4) % NY, 4))
     own_pay = pltpu.make_async_copy(pay.at[4], got.at[y], local_sem.at[4])
     own_pay.start()
     gate_copy = remote(gate_send, gate_sib, sib_s.at[3], sib_r.at[3], sibling)
@@ -488,7 +515,7 @@
     lax.fori_loop(0, last, send_hist, 0)
     own_pay.wait()
     take_in(7)
-    lax.fori_loop(0, NY, send_cands, 0)
+    send_cands()
     lax.fori_loop(last, NY, send_hist, 0)
 
     def wait_back(copy_sem, arr, back):
@@ -501,7 +528,7 @@
 
     def finish(arr, rows, at, inputs):
         half = rows // 2
-        low_half, low_rows = low_lanes(half), low_lanes(rows)
+        low_half = low_lanes(half)
         tiles, total = [], jnp.zeros((rows, 128), F32)
         for p in range(NY):
             at_p = 2 * ((p + NY // 2) % NY)
@@ -518,19 +545,20 @@
             squares = squares + t * t
         var = jnp.sum(squares, axis=1, keepdims=True) * (1.0 / D)
         scale = lax.rsqrt(var + NORM_EPS)
-        gated = []
-        for p in range(NY):
-            own = gate_own[p, at : at + rows].astype(F32)
-            sib = gate_sib[p, at : at + rows].astype(F32)
-            even, odd = jnp.where(is_first, own, sib), jnp.where(is_first, sib, own)
-            gate = jnp.where(low_rows, even, swap(odd))
-            g = tiles[p] * scale * gain_in[:, 128 * p : 128 * p + 128] * gate
-            gated.append(g.astype(BF16))
+        gated = [
+            (t * scale * gain_gate[at : at + rows, 128 * p : 128 * p + 128]).astype(BF16)
+            for p, t in enumerate(tiles)
+        ]
         result = dot(jnp.concatenate(gated, axis=1), out_w[...])
         return result + inputs.astype(F32)
 
     gate_copy.wait_recv()
     own_out_w.wait()
+    for p in range(NY):
+        own, sib = gate_own[p].astype(F32), gate_sib[p].astype(F32)
+        even, odd = jnp.where(is_first, own, sib), jnp.where(is_first, sib, own)
+        columns = slice(128 * p, 128 * p + 128)
+        gain_gate[:, columns] = join(even, odd) * gain_in[:, columns]
     wait_back((back_cs, back_cr), arr_c, back_c)
     cand_done = finish(arr_c, CR, HR, feats[2 * HR : 2 * HR + CR])
     split_rows(cand_done, done_send)
@@ -575,8 +603,12 @@
         return carry
 
     def pay_sends(t, carry):
-        pay_copy((t + 4) % NY).wait_send()
-        return carry
+        pay_copy(t).wait_send()
+        pay_copy(NY - t).wait_send()
+        return carry
+
+    first_hist.wait_send()
+    first_cand.wait_send()
 
     def back_sends(t, carry):
         to = (seq + t) % NS
@@ -585,7 +617,7 @@
         return carry
 
     lax.fori_loop(1, NU, user_sends, 0)
-    lax.fori_loop(1, NY, pay_sends, 0)
+    lax.fori_loop(1, NY // 2, pay_sends, 0)
     lax.fori_loop(1, NS, back_sends, 0)
 
 
@@ -602,6 +634,8 @@
         in_specs=[hbm] * 9,
         out_specs=(vmem, vmem),
         scratch_shapes=[
+            pltpu.VMEM((HR, D), BF16),
+            pltpu.VMEM((HR + CR, D), F32),
             pltpu.SMEM((1,), jnp.int32),
             pltpu.VMEM((1, 128), jnp.int32),
             pltpu.VMEM((32, D), BF16),
@@ -631,9 +665,9 @@
             pltpu.VMEM((NS, HR // 2, 128), BF16),
             pltpu.VMEM((512, 128), BF16),
             pltpu.VMEM((512, 128), BF16),
-            dma((12,)),
-            dma((2, 4, 2)),
-            dma((2, 4, 2)),
+            dma((13,)),
+            dma((2, 4, 4)),
+            dma((2, 4, 4)),
             dma((7, 2, 2)),
             dma((7, 2, 2)),
             dma((7, 2)),
@@ -652,21 +686,26 @@
             dma((NU,)),
         ],
         compiler_params=pltpu.CompilerParams(
-            collective_id=0, has_side_effects=True, vmem_limit_bytes=60 * 1024 * 1024
+            collective_id=0, has_side_effects=True, vmem_limit_bytes=48 * 1024 * 1024
         ),
         cost_estimate=pl.CostEstimate(
             flops=4 * 10**9, bytes_accessed=8 * 10**6, transcendentals=5 * 10**6
         ),
     )(
-        hist.reshape(HR, D),
-        length,
-        bucket,
-        cand,
-        owner.reshape(1, 32),
-        weight.reshape(D, 4 * DH),
-        bias,
-        gain.reshape(1, D),
-        out_weight,
+        *[
+            a if a is length else pltpu.with_memory_space_constraint(a, pltpu.HBM)
+            for a in (
+                hist.reshape(HR, D),
+                length,
+                bucket,
+                cand,
+                owner.reshape(1, 32),
+                weight.reshape(D, 4 * DH),
+                bias,
+                gain.reshape(1, D),
+                out_weight,
+            )
+        ]
     )
     return hist_out.reshape(1, HR, D), cand_out
 

time: 80.1 us -> 77 us (0.961); the launches traced: 79 us -> 76.8 us
  local copies, waits for them, and re-layouts: 3.14 us -> 1.33 us
    unnamed x2, local copies, waits for them, and re-layouts: 3.14 us -> 1.33 us
where the time goes in v3:
time: 77 us; the launch traced here: 76.8 us
  Pallas kernels  74.2 us (96%)
  local copies, waits for them, and re-layouts  1.33 us (2%)
  between operations  1.29 us (2%)
    pallas_call x1, Pallas kernels, body(): pl.pallas_call(kernel, out_shape=(jax.ShapeDtypeStruct((HR, D), BF16), ja...  74.2 us

profile of v3, /device:TPU:1, one launch (start us, length us, event | category | flops | bytes accessed | tf_op | source)
XLA Modules:
  0.0 76.8 jit_solution(3460783843387975427)
XLA Ops:
  1.3 74.2 %shard_map.104 = (bf16[128,1024]{1,0:T(8,128)(2,1)S(1)}, bf16[32,1024]{1,0:T(8,128)(2,1)S(1)}) custom-call(bf16[128,1024]{1,0:T(8,128)(2,1)} %bitcast.7, s32[1]{0:T(128)S(6)} %copy.13.length_hbm, s32[1,128]{1,0:T(1,128)} %bucket_hbm.1, bf16[32,1024]{1,0:T(8,128)(2,1)} %cand_hbm.1, s32[1,32]{1,0:T(1,128)} %bitcast.9, bf16[1024,256]{1,0:T(8,128)(2,1)} %bitcast.6, ...), custom_call_target="tpu_custom_call" | custom-call | flops 4000000000 | bytes 8000000 | tf_op jit(solution)/shard_map/pallas_call | solution.py:628
  75.5 0.7 copy.14
  76.2 0.6 copy.15

commit v4 on v3

--- a/solution.py
+++ b/solution.py
@@ -418,7 +418,7 @@
         queries[src, at + CR : at + 2 * CR] = jnp.where(low_c, swap(q_pair) * 0.0625, bias_lanes).astype(BF16)
 
     def source(m):
-        return (y + NY // 2 + jnp.where(m % 2 == 1, (m + 1) // 2, NY - m // 2)) % NY
+        return (y + NY // 2 + (0, 1, 7, 2, 6, 4, 3, 5)[m]) % NY
 
     def weigh(q, src, mask=None):
         w = half_silu(dot_nt(q, keys[src]))
@@ -446,7 +446,10 @@
     def take_in_step(step):
         pay_copy(NY - step).wait_recv()
         pay_copy(step).wait_recv()
-        take_in(2 * step - 1, 2 * step)
+        if step < 3:
+            take_in(2 * step - 1, 2 * step)
+        else:
+            take_in(6, 7)
 
     def back_c_copy(to):
         return remote(
@@ -510,11 +513,11 @@
     gate_copy = remote(gate_send, gate_sib, sib_s.at[3], sib_r.at[3], sibling)
     go(gate_copy)
     take_in_step(2)
+    own_pay.wait()
+    take_in(5)
+    last = jnp.where(source(6) < source(7), source(6), source(7))
+    lax.fori_loop(0, last, send_hist, 0)
     take_in_step(3)
-    last = source(7)
-    lax.fori_loop(0, last, send_hist, 0)
-    own_pay.wait()
-    take_in(7)
     send_cands()
     lax.fori_loop(last, NY, send_hist, 0)
 

time: 77 us -> 76.1 us (0.988)
  Pallas kernels: 74.2 us -> 73.4 us
    pallas_call x1, Pallas kernels: 74.2 us -> 73.4 us  [body(): pl.pallas_call(kernel, out_shape=(jax.ShapeDtypeStruct((HR, D), BF16), ja...]
where the time goes in v4:
time: 76.1 us; the launch traced here: 76 us
  Pallas kernels  73.4 us (96%)
  local copies, waits for them, and re-layouts  1.33 us (2%)
  between operations  1.29 us (2%)
    pallas_call x1, Pallas kernels, body(): pl.pallas_call(kernel, out_shape=(jax.ShapeDtypeStruct((HR, D), BF16), ja...  73.4 us

profile of v4, /device:TPU:1, one launch (start us, length us, event | category | flops | bytes accessed | tf_op | source)
XLA Modules:
  0.0 76.0 jit_solution(17342887511528078230)
XLA Ops:
  1.3 73.4 %shard_map.104 = (bf16[128,1024]{1,0:T(8,128)(2,1)S(1)}, bf16[32,1024]{1,0:T(8,128)(2,1)S(1)}) custom-call(bf16[128,1024]{1,0:T(8,128)(2,1)} %bitcast.7, s32[1]{0:T(128)S(6)} %copy.13.length_hbm, s32[1,128]{1,0:T(1,128)} %bucket_hbm.1, bf16[32,1024]{1,0:T(8,128)(2,1)} %cand_hbm.1, s32[1,32]{1,0:T(1,128)} %bitcast.9, bf16[1024,256]{1,0:T(8,128)(2,1)} %bitcast.6, ...), custom_call_target="tpu_custom_call" | custom-call | flops 4000000000 | bytes 8000000 | tf_op jit(solution)/shard_map/pallas_call | solution.py:631
  74.7 0.7 copy.14
  75.4 0.6 copy.15
